TPU v7x, 32 devices: a whole 2x2x4 slice. The times are simulated.
32 devices in a mesh: dp: 8 (over z, y), tensor: 4 (over x, core).
Axes of the slice: x: 2, y: 2, z: 4, core: 2. Of those that a mesh axis runs over, the one named last changes fastest.
Arguments:
- tokens: bfloat16 [32, 197, 768], P('dp'), may hold values from -6 to 6
- ln1_gain: float32 [768], replicated, may hold values from 0.5 to 1.5
- ln1_shift: float32 [768], replicated, may hold values from -1.75 to 1.75
- w_query: bfloat16 [768, 768], P(None, 'tensor'), may hold values from -0.21875 to 0.21875
- b_query: float32 [768], P('tensor'), may hold values from -1.25 to 1.25
- w_key: bfloat16 [768, 768], P(None, 'tensor'), may hold values from -0.21875 to 0.21875
- w_value: bfloat16 [768, 768], P(None, 'tensor'), may hold values from -0.21875 to 0.21875
- b_value: float32 [768], P('tensor'), may hold values from -1.25 to 1.25
- w_proj: bfloat16 [768, 768], P('tensor'), may hold values from -0.875 to 0.875
- b_proj: float32 [768], replicated, may hold values from -1.75 to 1.75
- ln2_gain: float32 [768], replicated, may hold values from 0.5 to 1.5
- ln2_shift: float32 [768], replicated, may hold values from -1.75 to 1.75
- w_fc1: bfloat16 [768, 3072], P(None, 'tensor'), may hold values from -0.21875 to 0.21875
- b_fc1: float32 [3072], P('tensor'), may hold values from -1.75 to 1.75
- w_fc2: bfloat16 [3072, 768], P('tensor'), may hold values from -0.109375 to 0.109375
- b_fc2: float32 [768], replicated, may hold values from -1.75 to 1.75
- cotangent: bfloat16 [32, 197, 768], P('dp'), may hold values from -6 to 6
Outputs:
- layer_out: bfloat16 [32, 197, 768], P('dp')
- tokens_grad: bfloat16 [32, 197, 768], P('dp')
- ln1_gain_grad: float32 [768], replicated
- ln1_shift_grad: float32 [768], replicated
- w_query_grad: float32 [768, 768], P(None, 'tensor')
- b_query_grad: float32 [768], P('tensor')
- w_key_grad: float32 [768, 768], P(None, 'tensor')
- w_value_grad: float32 [768, 768], P(None, 'tensor')
- b_value_grad: float32 [768], P('tensor')
- w_proj_grad: float32 [768, 768], P('tensor')
- b_proj_grad: float32 [768], replicated
- ln2_gain_grad: float32 [768], replicated
- ln2_shift_grad: float32 [768], replicated
- w_fc1_grad: float32 [768, 3072], P(None, 'tensor')
- b_fc1_grad: float32 [3072], P('tensor')
- w_fc2_grad: float32 [3072, 768], P('tensor')
- b_fc2_grad: float32 [768], replicated
All inputs are finite; a program needn't handle non-finite values.
Results may differ from a plain program's by a relative error of at most 0.012.
The roundings to bfloat16 on the way count: a program that leaves them out, or rounds other values in their place, can miss the bound.
Values may be sent and summed in bfloat16 or wider, within the bound.
A program may use at most 128 MiB of HBM per device.

v0:
```python
import jax
import jax.numpy as jnp
from jax import lax
from jax.sharding import PartitionSpec as P

HEAD_DIM = 64


EPSILON = 1e-06


def layer_norm(values, gain, shift):
    center = values - jnp.mean(values, axis=-1, keepdims=True)
    spread = jnp.mean(center * center, axis=-1, keepdims=True)
    return center * lax.rsqrt(spread + EPSILON) * gain + shift


def exact_gelu(values):
    return jax.nn.gelu(values, approximate=False)


def matmul(left, right):
    return jnp.dot(left, right, preferred_element_type=jnp.float32)


def inner_rows(left, right):
    return lax.dot_general(
        left, right, (((0,), (0,)), ((), ())), preferred_element_type=jnp.float32
    )


def times_transpose(left, right):
    return lax.dot_general(
        left, right, (((1,), (1,)), ((), ())), preferred_element_type=jnp.float32
    )


def attention_scores(query4, keys4, score_scale):
    return (
        jnp.einsum("bqhd,bkhd->bhqk", query4, keys4, preferred_element_type=jnp.float32)
        * score_scale
    )


def shards(
    tokens,
    ln1_gain,
    ln1_shift,
    w_query,
    b_query,
    w_key,
    w_value,
    b_value,
    w_proj,
    b_proj,
    ln2_gain,
    ln2_shift,
    w_fc1,
    b_fc1,
    w_fc2,
    b_fc2,
    cotangent,
):
    images, length, model_width = tokens.shape
    row_count = images * length
    local_width = w_query.shape[1]
    local_heads = local_width // HEAD_DIM
    score_scale = HEAD_DIM ** (-0.5)
    row_share = row_count // lax.axis_size("tensor")
    row_first = lax.axis_index("tensor") * row_share
    flat_rows = tokens.reshape(row_count, model_width).astype(jnp.float32)
    grad_rows = cotangent.reshape(row_count, model_width).astype(jnp.float32)
    shape4 = (images, length, local_heads, HEAD_DIM)
    normed = layer_norm(flat_rows, ln1_gain, ln1_shift).astype(jnp.bfloat16)
    query = (matmul(normed, w_query) + b_query).astype(jnp.bfloat16)
    keys = matmul(normed, w_key).astype(jnp.bfloat16)
    values = (matmul(normed, w_value) + b_value).astype(jnp.bfloat16)
    query4 = query.reshape(shape4)
    keys4 = keys.reshape(shape4)
    values4 = values.reshape(shape4)
    scores = attention_scores(query4, keys4, score_scale)
    highest = jnp.max(scores, axis=-1, keepdims=True)
    log_total = highest + jnp.log(jnp.sum(jnp.exp(scores - highest), axis=-1, keepdims=True))
    probs = jnp.exp(scores - log_total)
    mixed = jnp.einsum(
        "bhqk,bkhd->bqhd", probs.astype(jnp.bfloat16), values4, preferred_element_type=jnp.float32
    )
    mixed = mixed.reshape(row_count, local_width).astype(jnp.bfloat16)
    attn = lax.psum_scatter(matmul(mixed, w_proj), "tensor", scatter_dimension=0, tiled=True)
    resid = lax.dynamic_slice_in_dim(flat_rows, row_first, row_share, 0) + attn + b_proj
    middle = lax.all_gather(
        layer_norm(resid, ln2_gain, ln2_shift).astype(jnp.bfloat16), "tensor", axis=0, tiled=True
    )
    hidden = matmul(middle, w_fc1) + b_fc1
    active, gelu_back = jax.vjp(exact_gelu, hidden)
    active = active.astype(jnp.bfloat16)
    branch = lax.psum_scatter(
        matmul(active, w_fc2).astype(jnp.bfloat16), "tensor", scatter_dimension=0, tiled=True
    ).astype(jnp.float32)
    layer_out = lax.all_gather(
        (resid + branch + b_fc2).astype(jnp.bfloat16), "tensor", axis=0, tiled=True
    )
    layer_out = layer_out.reshape(tokens.shape)
    grad_low = grad_rows.astype(jnp.bfloat16)
    grad_fc2 = inner_rows(active, grad_low)
    grad_active = times_transpose(grad_low, w_fc2)
    grad_hidden = gelu_back(grad_active)[0].astype(jnp.bfloat16)
    grad_bfc1 = jnp.sum(grad_hidden.astype(jnp.float32), axis=0)
    grad_fc1 = inner_rows(middle, grad_hidden)
    grad_middle = lax.psum_scatter(
        times_transpose(grad_hidden, w_fc1), "tensor", scatter_dimension=0, tiled=True
    )
    own_grad = lax.dynamic_slice_in_dim(grad_rows, row_first, row_share, 0)
    unused, ln2_back = jax.vjp(layer_norm, resid, ln2_gain, ln2_shift)
    resid_part, grad_ln2_gain, grad_ln2_shift = ln2_back(grad_middle)
    grad_resid = own_grad + resid_part
    grad_bfc2 = jnp.sum(own_grad, axis=0)
    grad_bproj = jnp.sum(grad_resid, axis=0)
    resid_low = lax.all_gather(grad_resid.astype(jnp.bfloat16), "tensor", axis=0, tiled=True)
    grad_proj = inner_rows(mixed, resid_low)
    grad_mixed = times_transpose(resid_low, w_proj).astype(jnp.bfloat16).reshape(shape4)
    again = jnp.exp(attention_scores(query4, keys4, score_scale) - log_total)
    grad_values = jnp.einsum(
        "bhqk,bqhd->bkhd",
        again.astype(jnp.bfloat16),
        grad_mixed,
        preferred_element_type=jnp.float32,
    )
    grad_probs = jnp.einsum(
        "bqhd,bkhd->bhqk", grad_mixed, values4, preferred_element_type=jnp.float32
    )
    grad_scores = (
        again * (grad_probs - jnp.sum(again * grad_probs, axis=-1, keepdims=True))
    ).astype(jnp.bfloat16)
    grad_query = (
        jnp.einsum("bhqk,bkhd->bqhd", grad_scores, keys4, preferred_element_type=jnp.float32)
        * score_scale
    )
    grad_keys = (
        jnp.einsum("bhqk,bqhd->bkhd", grad_scores, query4, preferred_element_type=jnp.float32)
        * score_scale
    )
    grad_query = grad_query.reshape(row_count, local_width).astype(jnp.bfloat16)
    grad_keys = grad_keys.reshape(row_count, local_width).astype(jnp.bfloat16)
    grad_values = grad_values.reshape(row_count, local_width).astype(jnp.bfloat16)
    grad_bquery = jnp.sum(grad_query.astype(jnp.float32), axis=0)
    grad_bvalue = jnp.sum(grad_values.astype(jnp.float32), axis=0)
    grad_wquery = inner_rows(normed, grad_query)
    grad_wkey = inner_rows(normed, grad_keys)
    grad_wvalue = inner_rows(normed, grad_values)
    part_query = times_transpose(grad_query, w_query)
    part_keys = times_transpose(grad_keys, w_key)
    part_values = times_transpose(grad_values, w_value)
    grad_normed = lax.psum_scatter(
        part_query + part_keys + part_values, "tensor", scatter_dimension=0, tiled=True
    )
    own_rows = lax.dynamic_slice_in_dim(flat_rows, row_first, row_share, 0)
    unused_one, ln1_back = jax.vjp(layer_norm, own_rows, ln1_gain, ln1_shift)
    input_part, grad_ln1_gain, grad_ln1_shift = ln1_back(grad_normed)
    tokens_grad = lax.all_gather(
        (grad_resid + input_part).astype(jnp.bfloat16), "tensor", axis=0, tiled=True
    )
    matrices = lax.psum(
        (
            grad_wquery,
            grad_bquery,
            grad_wkey,
            grad_wvalue,
            grad_bvalue,
            grad_proj,
            grad_fc1,
            grad_bfc1,
            grad_fc2,
        ),
        "dp",
    )
    (
        grad_wquery,
        grad_bquery,
        grad_wkey,
        grad_wvalue,
        grad_bvalue,
        grad_proj,
        grad_fc1,
        grad_bfc1,
        grad_fc2,
    ) = matrices
    smalls = lax.psum(
        (grad_ln1_gain, grad_ln1_shift, grad_bproj, grad_ln2_gain, grad_ln2_shift, grad_bfc2),
        ("dp", "tensor"),
    )
    grad_ln1_gain, grad_ln1_shift, grad_bproj, grad_ln2_gain, grad_ln2_shift, grad_bfc2 = smalls
    tokens_grad = tokens_grad.reshape(tokens.shape)
    return (
        layer_out,
        tokens_grad,
        grad_ln1_gain,
        grad_ln1_shift,
        grad_wquery,
        grad_bquery,
        grad_wkey,
        grad_wvalue,
        grad_bvalue,
        grad_proj,
        grad_bproj,
        grad_ln2_gain,
        grad_ln2_shift,
        grad_fc1,
        grad_bfc1,
        grad_fc2,
        grad_bfc2,
    )


def solution(mesh):
    in_specs = (
        P("dp", None, None),
        P(),
        P(),
        P(None, "tensor"),
        P("tensor"),
        P(None, "tensor"),
        P(None, "tensor"),
        P("tensor"),
        P("tensor", None),
        P(),
        P(),
        P(),
        P(None, "tensor"),
        P("tensor"),
        P("tensor", None),
        P(),
        P("dp", None, None),
    )
    out_specs = (
        P("dp", None, None),
        P("dp", None, None),
        P(),
        P(),
        P(None, "tensor"),
        P("tensor"),
        P(None, "tensor"),
        P(None, "tensor"),
        P("tensor"),
        P("tensor", None),
        P(),
        P(),
        P(),
        P(None, "tensor"),
        P("tensor"),
        P("tensor", None),
        P(),
    )
    return jax.shard_map(shards, mesh=mesh, in_specs=in_specs, out_specs=out_specs, check_vma=False)
```

profile of v0, /device:TPU:0, one launch (start us, length us, event | category | flops | bytes accessed | tf_op | source)
XLA Modules:
  0.0 534.8 jit_solution(16166628521108999006)
XLA Ops:
  7.3 3.1 copy.96
  12.1 3.4 reshape.246
  15.9 2.1 add_convert_fusion.1
  18.0 1.4 fusion.13
  19.4 1.3 reshape.239
  20.7 2.3 convolution_convert_fusion.4
  23.1 1.3 reshape.241
  24.4 2.5 fusion.14
  26.9 1.3 reshape.240
  30.9 2.0 fusion.45
  32.9 27.9 %fusion = f32[200,768]{1,0:T(8,128)S(1)} fusion(f32[788,768]{1,0:T(8,128)} %fusion.45), kind=kCustom, calls=%all-reduce-scatter | all-reduce-scatter fusion | flops 614401 | bytes 3035648
  60.8 1.3 collective-permute-start
  65.1 1.4 fusion.43
  67.9 1.4 copy.105
  69.3 1.4 reshape.243
  70.7 16.8 %all-gather.9.cloned.1.call-done = bf16[4,197,768]{2,1,0:T(8,128)(2,1)} async-done(((bf16[1,197,768]{2,1,0:T(8,128)(2,1)}), bf16[4,197,768]{2,1,0:T(8,128)(2,1)}) %all-gather.9.cloned.1.call-update) | async-done | bytes 1210384 | tf_op jit(solution)/shard_map/all_gather | solution.py:91
  87.5 2.6 reshape.248
  90.1 2.9 fusion.46
  93.0 8.2 %convert_reduce_fusion = (f32[768]{0:T(1024)}, bf16[788,768]{1,0:T(8,128)(2,1)S(1)}, f32[788,768]{1,0:T(8,128)}) fusion(f32[788,768]{1,0:T(8,128)S(1)} %fusion.46, f32[768]{0:T(1024)S(1)} %copy-done.37, bf16[788,768]{1,0:T(8,128)(2,1)S(1)} %copy-done.18, bf16[768,768]{1,0:T(8,128)(2,1)S(1)} %copy-done), kind=kOutput, calls=%fused_computation.6 | convolution fusion | flops 974950656 | bytes 8448000 | tf_op jit(solution)/shard_map/dot_general | solution.py:33
  102.3 2.6 fusion.47
  104.8 25.6 %fusion.2 = f32[200,768]{1,0:T(8,128)S(1)} fusion(f32[788,768]{1,0:T(8,128)} %fusion.47), kind=kCustom, calls=%all-reduce-scatter.2 | all-reduce-scatter fusion | flops 614401 | bytes 3035648
  130.5 1.9 collective-permute-start.2
  132.4 2.8 multiply_convert_fusion.1
  136.2 2.1 convolution_convert_fusion
  138.4 17.2 %fusion.1 = bf16[200,768]{1,0:T(8,128)(2,1)S(1)} fusion(bf16[788,768]{1,0:T(8,128)(2,1)} %convolution_convert_fusion), kind=kCustom, calls=%all-reduce-scatter.1 | all-reduce-scatter fusion | flops 614401 | bytes 1518080
  155.6 1.3 collective-permute-start.1
  158.2 1.2 concatenate.2
  160.9 1.8 convert_bitcast_fusion
  163.8 20.2 %all-gather.13.cloned.1.call-done = bf16[4,197,768]{2,1,0:T(8,128)(2,1)} async-done(((bf16[1,197,768]{2,1,0:T(8,128)(2,1)}), bf16[4,197,768]{2,1,0:T(8,128)(2,1)}) %all-gather.13.cloned.1.call-update) | async-done | bytes 1210384 | tf_op jit(solution)/shard_map/all_gather | solution.py:119
  184.0 2.7 reshape.252
  186.7 2.7 convolution_convert_fusion.3
  189.4 2.1 reshape.244
  191.5 1.8 multiply_reduce_fusion
  194.8 1.3 fusion.17
  196.0 1.3 convert_reduce_fusion.2
  198.0 1.6 fusion.48
  199.6 2.0 copy.113
  201.7 2.1 convert_element_type.151
  203.7 3.1 fusion.49
  207.9 1.3 convert_element_type.154
  209.2 3.8 add_add_fusion
  213.0 26.4 %fusion.3 = f32[200,768]{1,0:T(8,128)} fusion(f32[788,768]{1,0:T(8,128)} %add_add_fusion), kind=kCustom, calls=%all-reduce-scatter.3 | all-reduce-scatter fusion | flops 614401 | bytes 3035648
  240.3 1.3 collective-permute-start.3
  242.4 3.5 concatenate.3
  245.9 1.5 multiply_reduce_fusion.4
  247.4 1.4 fusion.41
  248.8 2.0 convert_reduce_fusion.4
  251.2 2.1 add_convert_fusion.2
  253.8 4.7 fusion.54
  258.5 2.9 fusion.55
  261.3 1.3 fusion.50
  262.6 1.3 fusion.51
  263.9 1.3 fusion.52
  265.2 1.3 fusion.53
  266.7 2.8 copy.119
  269.5 22.5 %all-reduce.9 = (f32[192]{0:T(256)}, f32[192]{0:T(256)}, f32[768]{0:T(1024)}) all-reduce(f32[192]{0:T(256)S(1)} %reduce_sum.248, f32[192]{0:T(256)S(1)} %reduce_sum.250, f32[768]{0:T(1024)S(1)} %copy-done.39), channel_id=1, replica_groups=mesh['dp'=8,'tensor'=4] {'dp'}, use_global_device_ids=true, to_apply=%region_23.0 | all-reduce | flops 1152 | bytes 9216 | tf_op jit(solution)/shard_map/psum | solution.py:163
  292.0 45.3 %all-reduce.8 = (f32[768]{0:T(1024)}, f32[768]{0:T(1024)}, f32[768]{0:T(1024)}, f32[768]{0:T(1024)}, f32[768]{0:T(1024)}, /*index=5*/f32[768]{0:T(1024)}) all-reduce(f32[768]{0:T(1024)S(1)} %get-tuple-element.85, f32[768]{0:T(1024)S(1)} %get-tuple-element.92, ...), channel_id=1, replica_groups=mesh['dp'=8,'tensor'=4] {'dp','tensor'}, use_global_device_ids=true, to_apply=%region_18.0 | all-reduce | flops 4608 | bytes 36864 | tf_op jit(solution)/shard_map/psum | solution.py:188
  337.3 2.8 copy.120
  340.1 177.5 %all-reduce.13.cloned.1.call-done = (f32[768,192]{0,1:T(8,128)}, f32[768,192]{0,1:T(8,128)}, f32[768,192]{0,1:T(8,128)}, f32[192,768]{1,0:T(8,128)}, f32[768,768]{1,0:T(8,128)}, /*index=5*/f32[768,768]{1,0:T(8,128)}) async-done(((f32[768,192]{0,1:T(8,128)}, f32[768,192]{0,1:T(8,128)}, f32[768,192]{0,1:T(8,128)}, f32[192,768]{1,0:T(8,128)}, f32[768,768]{1,0:T(8,128)}, /*index=5*/f32[768,768]{1,0:T(8,128)}), ...) | async-done | bytes 7077904 | tf_op jit(solution)/shard_map/psum | solution.py:163
  517.6 2.1 copy.161
  519.7 1.9 copy.162
  521.6 1.9 copy.163
  524.3 1.4 copy.165
  526.9 1.4 copy.166
  (150 shorter events, 22.0 us)
Async XLA Ops:
  7.2 85.8 %copy-start = (bf16[768,768]{1,0:T(8,128)(2,1)S(1)}, bf16[768,768]{1,0:T(8,128)(2,1)}, u32[]{:S(2)}) copy-start(bf16[768,768]{1,0:T(8,128)(2,1)} %param.31) | copy-start | bytes 3538948
  7.2 3.1 copy-start.5
  7.2 80.3 %all-gather.9.cloned.1.call-start = ((), (), s32[]{:S(2)}) async-start(), calls=%async_computation | async-start | bytes 1536000 | tf_op jit(solution)/shard_map/all_gather | solution.py:91
  10.9 4.7 copy-start.23
  12.1 3.7 copy-start.32
  12.1 3.7 copy-start.34
  15.6 2.4 copy-start.31
  15.6 2.4 copy-start.42
  15.6 3.8 copy-start.28
  18.0 6.4 %copy-start.43 = (f32[192]{0:T(256)S(1)}, f32[192]{0:T(256)}, u32[]{:S(2)}) copy-start(f32[192]{0:T(256)} %param.21) | copy-start | bytes 2308
  24.4 4.4 copy-start.8
  28.2 1.1 copy-start.10
  28.8 1.4 copy-start.2
  29.3 1.5 copy-start.30
  30.8 29.9 %copy-start.13 = (bf16[788,192]{0,1:T(8,128)(2,1)}, bf16[788,192]{0,1:T(8,128)(2,1)S(1)}, u32[]{:S(2)}) copy-start(bf16[788,192]{0,1:T(8,128)(2,1)S(1)} %convert_element_type.135) | copy-start | bytes 907780
  32.9 30.5 %copy-start.40 = (u32[32]{0:T(128)S(1)}, u32[32]{0:T(128)}, u32[]{:S(2)}) copy-start(u32[32]{0:T(128)} %constant.100) | copy-start | bytes 388
  32.9 32.2 %copy-start.35 = (f32[768]{0:T(1024)S(1)}, f32[768]{0:T(1024)}, u32[]{:S(2)}) copy-start(f32[768]{0:T(1024)} %param.26) | copy-start | bytes 9220
  60.8 6.0 %copy-start.33 = (f32[768]{0:T(1024)S(1)}, f32[768]{0:T(1024)}, u32[]{:S(2)}) copy-start(f32[768]{0:T(1024)} %param.27) | copy-start | bytes 9220
  60.8 6.0 %copy-start.36 = (f32[768]{0:T(1024)S(1)}, f32[768]{0:T(1024)}, u32[]{:S(2)}) copy-start(f32[768]{0:T(1024)} %param.28) | copy-start | bytes 9220
  60.8 3.8 collective-permute-start
  67.7 116.3 %all-gather.13.cloned.1.call-start = ((), (), s32[]{:S(2)}) async-start(), calls=%async_computation.2 | async-start | bytes 1536000 | tf_op jit(solution)/shard_map/all_gather | solution.py:119
  90.1 2.9 copy-start.18
  90.1 2.9 copy-start.37
  93.0 8.2 %copy-start.20 = (f32[788,768]{1,0:T(8,128)}, f32[788,768]{1,0:T(8,128)S(1)}, u32[]{:S(2)}) copy-start(f32[788,768]{1,0:T(8,128)S(1)} %fusion.46) | copy-start | bytes 7262212
  93.0 9.2 %copy-start.41 = (bf16[768,768]{1,0:T(8,128)(2,1)S(1)}, bf16[768,768]{1,0:T(8,128)(2,1)}, u32[]{:S(2)}) copy-start(bf16[768,768]{1,0:T(8,128)(2,1)} %param.29) | copy-start | bytes 3538948
  101.3 1.0 copy-start.44
  130.5 27.7 %collective-permute-start.2 = (f32[9,768]{1,0:T(8,128)S(1)}, f32[9,768]{1,0:T(8,128)}, u32[]{:S(2)}, u32[]{:S(2)}) collective-permute-start(f32[9,768]{1,0:T(8,128)S(1)} %slice.2), channel_id=1, source_target_pairs={{0,1},{1,2},{2,3},{4,5},{5,6},{6,7},{8,9},{9,10},{10,11},{12,13},{... | collective-permute-start | bytes 82952
  135.1 1.1 copy-start.26
  138.4 21.4 %copy-start.38 = (f32[768]{0:T(1024)S(1)}, f32[768]{0:T(1024)}, u32[]{:S(2)}) copy-start(f32[768]{0:T(1024)} %param.32) | copy-start | bytes 9220
  155.6 2.1 collective-permute-start.1
  162.7 104.0 %all-gather.11.cloned.1.call-start = ((), (), s32[]{:S(2)}) async-start(), calls=%async_computation.1 | async-start | bytes 1536000 | tf_op jit(solution)/shard_map/all_gather | solution.py:100
  163.5 28.0 %copy-start.3 = (f32[4,3,197,197]{2,3,1,0:T(8,128)S(1)}, f32[4,3,197,197]{2,3,1,0:T(8,128)}, u32[]{:S(2)}) copy-start(f32[4,3,197,197]{2,3,1,0:T(8,128)} %copy-done.2) | copy-start | bytes 5588500
  163.5 173.8 %all-gather.15.cloned.1.call-start = ((), (), s32[]{:S(2)}) async-start(), calls=%async_computation.3 | async-start | bytes 1536000 | tf_op jit(solution)/shard_map/all_gather | solution.py:160
  193.3 1.0 copy-start.9
  193.3 1.4 copy-start.11
  194.3 1.7 copy-start.12
  198.0 8.9 %copy-start.15 = (bf16[788,192]{0,1:T(8,128)(2,1)}, bf16[788,192]{0,1:T(8,128)(2,1)S(1)}, u32[]{:S(2)}) copy-start(bf16[788,192]{0,1:T(8,128)(2,1)S(1)} %convert_element_type.148) | copy-start | bytes 907780
  203.7 3.1 copy-start.25
  213.0 32.9 %copy-start.4 = (f32[788,768]{1,0:T(8,128)S(1)}, f32[788,768]{1,0:T(8,128)}, u32[]{:S(2)}) copy-start(f32[788,768]{1,0:T(8,128)} %reshape.246) | copy-start | bytes 7262212
  240.3 2.1 collective-permute-start.3
  245.9 5.3 copy-start.24
  248.8 2.4 copy-start.6
  250.9 266.7 %all-reduce.13.cloned.1.call-start = ((), (), s32[]{:S(2)}) async-start(), calls=%async_computation.4 | async-start | bytes 14155776 | tf_op jit(solution)/shard_map/psum | solution.py:163
  253.8 4.7 copy-start.19
  253.8 4.7 copy-start.27
  258.5 2.9 copy-start.16
  258.5 4.2 copy-start.17
  262.6 2.6 copy-start.7
  262.6 2.6 copy-start.14
  266.6 3.0 copy-start.39
  517.6 5.9 %copy-start.29 = (f32[192,768]{1,0:T(8,128)S(1)}, f32[192,768]{1,0:T(8,128)}, u32[]{:S(2)}) copy-start(f32[192,768]{1,0:T(8,128)} %get-tuple-element.137) | copy-start | bytes 1769476
  517.6 6.7 %copy-start.22 = (f32[768,768]{1,0:T(8,128)S(1)}, f32[768,768]{1,0:T(8,128)}, u32[]{:S(2)}) copy-start(f32[768,768]{1,0:T(8,128)} %get-tuple-element.141) | copy-start | bytes 7077892
  524.3 2.5 copy-start.21
  524.3 3.9 copy-start.1
Sparse Core Ops, SparseCore 0:
  67.8 19.6 all-gather.8
  162.9 21.0 all-gather.12
  185.6 17.7 all-gather.10
  251.0 22.0 all-gather.14
  279.2 238.3 all-reduce.12
where the time goes:
time: 537 us; the launch traced here: 535 us
  waiting for transfers between devices  217 us (40%)
  blocking collectives  165 us (31%)
  local copies, waits for them, and re-layouts  55.6 us (10%)
  matrix products  53.8 us (10%)
  other arithmetic  21.8 us (4%)
  between operations  15.1 us (3%)
  starting transfers between devices  6.63 us (1%)
    psum x1, waiting for transfers between devices, shards(): lax.psum((grad_wquery, grad_bquery, grad_wkey, grad_wvalue, grad_bvalue,...  178 us
    unnamed x4, blocking collectives  97.1 us
    psum x1, blocking collectives, shards(): lax.psum((grad_ln1_gain, grad_ln1_shift, grad_bproj, grad_ln2_gain, grad_...  45.3 us
    unnamed x112, local copies, waits for them, and re-layouts  33.1 us
    psum x1, blocking collectives, shards(): lax.psum((grad_wquery, grad_bquery, grad_wkey, grad_wvalue, grad_bvalue,...  22.5 us
    dot_general x6, matrix products, times_transpose(): lax.dot_general(left, right, (((1,), (1,)), ((), ())), preferred_element_...  21.9 us
    all_gather x1, waiting for transfers between devices, shards(): lax.all_gather(grad_resid.astype(jnp.bfloat16), 'tensor', axis=0, tiled=T...  20.2 us
    all_gather x1, waiting for transfers between devices, shards(): lax.all_gather(layer_norm(resid, ln2_gain, ln2_shift).astype(jnp.bfloat16...  16.8 us
  transfers between devices with their start and end apart: 9, of which 5 were waited for; matrix products, arithmetic and copies ran while one was open for 21% of the time, Pallas kernels for 0%

commit v1 on v0

v1 whole, which is shorter than its diff:
```python
import jax
import jax.numpy as jnp
from jax import lax
from jax.experimental import pallas as pl
from jax.experimental.pallas import tpu as pltpu
from jax.sharding import PartitionSpec as P

HEAD_DIM = 64
EPSILON = 1e-06
BF16 = jnp.bfloat16
F32 = jnp.float32
MESH = pl.DeviceIdType.MESH
VMEM_LIMIT = 56 * 1024 * 1024


def matmul(left, right):
    return jnp.dot(left, right, preferred_element_type=F32)


def inner_rows(left, right):
    return lax.dot_general(left, right, (((0,), (0,)), ((), ())), preferred_element_type=F32)


def times_transpose(left, right):
    return lax.dot_general(left, right, (((1,), (1,)), ((), ())), preferred_element_type=F32)


def normalize(values):
    center = values - jnp.mean(values, axis=-1, keepdims=True)
    scale = lax.rsqrt(jnp.mean(center * center, axis=-1, keepdims=True) + EPSILON)
    return center * scale, scale


def norm_back(hat, scale, gain, grad):
    inner = grad * gain
    return scale * (
        inner
        - jnp.mean(inner, axis=-1, keepdims=True)
        - hat * jnp.mean(inner * hat, axis=-1, keepdims=True)
    )


def soft_probs(query, keys, length):
    scores = times_transpose(query, keys) * (HEAD_DIM**-0.5)
    column = lax.broadcasted_iota(jnp.int32, scores.shape, 1)
    scores = jnp.where(column < length, scores, -1e30)
    raised = jnp.exp(scores - jnp.max(scores, axis=-1, keepdims=True))
    return raised * (1.0 / jnp.sum(raised, axis=-1, keepdims=True))


def attention_kernel(
    length, x_ref, gain, shift, wq, bq, wk, wv, bv, wp, a_ref, q_ref, k_ref, v_ref, o_ref, part_ref
):
    hat, _ = normalize(x_ref[0].astype(F32))
    normed = (hat * gain[...] + shift[...]).astype(BF16)
    a_ref[0] = normed
    query = (matmul(normed, wq[...]) + bq[...]).astype(BF16)
    keys = matmul(normed, wk[...]).astype(BF16)
    values = (matmul(normed, wv[...]) + bv[...]).astype(BF16)
    q_ref[0] = query
    k_ref[0] = keys
    v_ref[0] = values
    heads = []
    for head in range(query.shape[1] // HEAD_DIM):
        span = slice(head * HEAD_DIM, (head + 1) * HEAD_DIM)
        probs = soft_probs(query[:, span], keys[:, span], length)
        heads.append(matmul(probs.astype(BF16), values[:, span]))
    mixed = jnp.concatenate(heads, axis=1).astype(BF16)
    o_ref[0] = mixed
    part_ref[0] = matmul(mixed, wp[...]).astype(BF16)


def feed_kernel(c_ref, g_ref, w1, b1, w2, part_ref, fc_ref, bias_ref, acc1, acc2):
    step = pl.program_id(0)
    rows = c_ref.shape[1]
    width = c_ref.shape[2]

    @pl.when(step == 0)
    def _():
        acc1[...] = jnp.zeros_like(acc1)
        acc2[...] = jnp.zeros_like(acc2)
        bias_ref[...] = jnp.zeros_like(bias_ref)

    middle = c_ref[0]
    grad = g_ref[0]
    hidden = matmul(middle, w1[...]) + b1[...]
    cdf = 0.5 * (1.0 + lax.erf(hidden * (0.5**0.5)))
    slope = cdf + hidden * jnp.exp(-0.5 * hidden * hidden) * 0.3989422804014327
    active = (hidden * cdf).astype(BF16)
    grad_hidden = (times_transpose(grad, w2[...]) * slope).astype(BF16)
    part_ref[0, :rows] = matmul(active, w2[...]).astype(BF16)
    part_ref[0, rows:] = times_transpose(grad_hidden, w1[...]).astype(BF16)
    acc2[...] += inner_rows(active, grad)
    acc1[...] += inner_rows(middle, grad_hidden)
    bias_ref[...] += jnp.sum(grad_hidden.astype(F32), axis=0, keepdims=True)

    @pl.when(step == pl.num_programs(0) - 1)
    def _():
        fc_ref[:width] = acc1[...].astype(BF16)
        fc_ref[width:] = acc2[...].astype(BF16)


def back_kernel(
    length, h_ref, o_ref, a_ref, q_ref, k_ref, v_ref, wp, wq, wk, wv,
    part_ref, gq_ref, gk_ref, gv_ref, gp_ref, bq_ref, bv_ref, accq, acck, accv, accp,
):
    step = pl.program_id(0)

    @pl.when(step == 0)
    def _():
        for ref in (accq, acck, accv, accp, bq_ref, bv_ref):
            ref[...] = jnp.zeros_like(ref)

    low = h_ref[0]
    accp[...] += inner_rows(o_ref[0], low)
    grad_mixed = times_transpose(low, wp[...]).astype(BF16)
    normed = a_ref[0]
    query, keys, values = q_ref[0], k_ref[0], v_ref[0]
    score_scale = HEAD_DIM**-0.5
    dq, dk, dv = [], [], []
    for head in range(query.shape[1] // HEAD_DIM):
        span = slice(head * HEAD_DIM, (head + 1) * HEAD_DIM)
        qh, kh, vh, gh = query[:, span], keys[:, span], values[:, span], grad_mixed[:, span]
        probs = soft_probs(qh, kh, length)
        dv.append(inner_rows(probs.astype(BF16), gh))
        grad_probs = times_transpose(gh, vh)
        total = jnp.sum(probs * grad_probs, axis=-1, keepdims=True)
        grad_scores = (probs * (grad_probs - total)).astype(BF16)
        dq.append(matmul(grad_scores, kh) * score_scale)
        dk.append(inner_rows(grad_scores, qh) * score_scale)
    dq = jnp.concatenate(dq, axis=1).astype(BF16)
    dk = jnp.concatenate(dk, axis=1).astype(BF16)
    dv = jnp.concatenate(dv, axis=1).astype(BF16)
    bq_ref[...] += jnp.sum(dq.astype(F32), axis=0, keepdims=True)
    bv_ref[...] += jnp.sum(dv.astype(F32), axis=0, keepdims=True)
    part_ref[0] = (
        times_transpose(dq, wq[...]) + times_transpose(dk, wk[...]) + times_transpose(dv, wv[...])
    ).astype(BF16)
    accq[...] += inner_rows(normed, dq)
    acck[...] += inner_rows(normed, dk)
    accv[...] += inner_rows(normed, dv)

    @pl.when(step == pl.num_programs(0) - 1)
    def _():
        gq_ref[...] = accq[...].astype(BF16)
        gk_ref[...] = acck[...].astype(BF16)
        gv_ref[...] = accv[...].astype(BF16)
        gp_ref[...] = accp[...].astype(BF16)


def places():
    here = lax.axis_index("tensor")
    return here, here + 1 - 2 * (here % 2), (here + 2) % 4, 3 - here


def greet(near, far):
    barrier = pltpu.get_barrier_semaphore()
    for other in (near, far):
        pl.semaphore_signal(barrier, inc=1, device_id={"tensor": other}, device_id_type=MESH)
    pl.semaphore_wait(barrier, 2)


def send(src, dst, sems, slot, other):
    copy = pltpu.make_async_remote_copy(
        src_ref=src,
        dst_ref=dst,
        send_sem=sems.at[0, slot],
        recv_sem=sems.at[1, slot],
        device_id={"tensor": other},
        device_id_type=MESH,
    )
    copy.start()
    return copy


def reduce_share(part, near_in, out_buf, far_in, sems):
    here, near, far, diag = places()
    first = send(part.at[diag], near_in.at[0], sems, 0, near)
    second = send(part.at[near], near_in.at[1], sems, 1, near)
    first.wait_recv()
    out_buf[...] = (part[far].astype(F32) + near_in[0].astype(F32)).astype(BF16)
    third = send(out_buf, far_in, sems, 2, far)
    second.wait_recv()
    near_sum = part[here].astype(F32) + near_in[1].astype(F32)
    third.wait_recv()
    total = near_sum + far_in[...].astype(F32)
    first.wait_send()
    second.wait_send()
    third.wait_send()
    return total


def gather_share(out, sems):
    here, near, far, diag = places()
    first = send(out.at[here], out.at[here], sems, 3, far)
    second = send(out.at[here], out.at[here], sems, 4, near)
    first.wait_recv()
    third = send(out.at[far], out.at[far], sems, 5, near)
    second.wait_recv()
    third.wait_recv()
    first.wait_send()
    second.wait_send()
    third.wait_send()


def middle_kernel(part, x_ref, bias, gain, shift, out, h_ref, near_in, out_buf, far_in, sems):
    here, near, far, _ = places()
    greet(near, far)
    total = reduce_share(part, near_in, out_buf, far_in, sems)
    resid = x_ref[here].astype(F32) + total + bias[...]
    h_ref[...] = resid
    hat, _ = normalize(resid)
    out[here] = (hat * gain[...] + shift[...]).astype(BF16)
    gather_share(out, sems)


def turn_kernel(
    part, h_ref, g_ref, bias, gain, out, dh_ref, small, near_in, out_buf, far_in, sems
):
    here, near, far, _ = places()
    rows = h_ref.shape[0]
    greet(near, far)
    total = reduce_share(part, near_in, out_buf, far_in, sems)
    resid = h_ref[...]
    grad = total[rows:]
    own = g_ref[here].astype(F32)
    hat, scale = normalize(resid)
    grad_resid = own + norm_back(hat, scale, gain[...], grad)
    dh_ref[...] = grad_resid
    out[here, :rows] = (resid + total[:rows] + bias[...]).astype(BF16)
    out[here, rows:] = grad_resid.astype(BF16)
    small[0:1] = jnp.sum(grad * hat, axis=0, keepdims=True)
    small[1:2] = jnp.sum(grad, axis=0, keepdims=True)
    small[2:3] = jnp.sum(grad_resid, axis=0, keepdims=True)
    small[3:4] = jnp.sum(own, axis=0, keepdims=True)
    small[4:8] = jnp.zeros((4, small.shape[1]), F32)
    gather_share(out, sems)


def last_kernel(
    part, x_ref, dh_ref, gain, small_in, out, small, near_in, out_buf, far_in, sums, got, sems
):
    here, near, far, _ = places()
    greet(near, far)
    total = reduce_share(part, near_in, out_buf, far_in, sems)
    hat, scale = normalize(x_ref[here].astype(F32))
    out[here] = (dh_ref[...] + norm_back(hat, scale, gain[...], total)).astype(BF16)
    sums[0] = small_in[...]
    sums[0, 4:5] = jnp.sum(total * hat, axis=0, keepdims=True)
    sums[0, 5:6] = jnp.sum(total, axis=0, keepdims=True)
    one = send(sums.at[0], got.at[0], sems, 6, near)
    gather_share(out, sems)
    one.wait()
    sums[1] = sums[0] + got[0]
    two = send(sums.at[1], got.at[1], sems, 7, far)
    two.wait()
    small[...] = sums[1] + got[1]


def whole(count):
    return [pl.BlockSpec(memory_space=pltpu.VMEM)] * count


def fixed(shape):
    return pl.BlockSpec(shape, lambda step: (0,) * len(shape))


def each(shape):
    return pl.BlockSpec((1,) + shape[1:], lambda step: (step,) + (0,) * (len(shape) - 1))


def struct(shape, dtype):
    return jax.ShapeDtypeStruct(shape, dtype)


def exchange(kernel, number, name, outs, rows, width, extra, args):
    return pl.pallas_call(
        kernel,
        out_shape=outs,
        in_specs=whole(len(args)),
        out_specs=whole(len(outs)),
        scratch_shapes=[
            pltpu.VMEM((2, rows, width), BF16),
            pltpu.VMEM((rows, width), BF16),
            pltpu.VMEM((rows, width), BF16),
            *extra,
            pltpu.SemaphoreType.DMA((2, 8)),
        ],
        compiler_params=pltpu.CompilerParams(
            collective_id=number, has_side_effects=True, vmem_limit_bytes=VMEM_LIMIT
        ),
        cost_estimate=pl.CostEstimate(
            flops=0, bytes_accessed=50_000_000, transcendentals=0
        ),
        name=name,
    )(*args)


def stepped(kernel, name, steps, args, arg_specs, outs, out_specs, scratch, flops):
    return pl.pallas_call(
        kernel,
        grid=(steps,),
        out_shape=outs,
        in_specs=arg_specs,
        out_specs=out_specs,
        scratch_shapes=scratch,
        compiler_params=pltpu.CompilerParams(vmem_limit_bytes=VMEM_LIMIT),
        cost_estimate=pl.CostEstimate(
            flops=flops, bytes_accessed=20_000_000, transcendentals=0
        ),
        name=name,
    )(*args)


def partners(count, distance):
    return [(i, i ^ distance) for i in range(count)]


def sum_images(array):
    count = lax.axis_size("dp")
    me = lax.axis_index("dp")
    distances = []
    distance = 1
    while distance < count:
        distances.append(distance)
        distance *= 2
    current = array
    for distance in distances:
        half = current.shape[0] // 2
        bit = (me // distance) % 2
        keep = lax.dynamic_slice_in_dim(current, bit * half, half, 0)
        give = lax.dynamic_slice_in_dim(current, (1 - bit) * half, half, 0)
        got = lax.ppermute(give.astype(BF16), "dp", partners(count, distance))
        current = keep.astype(F32) + got.astype(F32)
    current = current.astype(BF16)
    for distance in reversed(distances):
        bit = (me // distance) % 2
        got = lax.ppermute(current, "dp", partners(count, distance))
        current = jnp.where(
            bit == 0,
            jnp.concatenate([current, got], axis=0),
            jnp.concatenate([got, current], axis=0),
        )
    return current


def sum_small(array):
    count = lax.axis_size("dp")
    distance = 1
    while distance < count:
        array = array + lax.ppermute(array, "dp", partners(count, distance))
        distance *= 2
    return array


def shards(
    tokens, ln1_gain, ln1_shift, w_query, b_query, w_key, w_value, b_value, w_proj, b_proj,
    ln2_gain, ln2_shift, w_fc1, b_fc1, w_fc2, b_fc2, cotangent,
):
    images, length, width = tokens.shape
    assert images == lax.axis_size("tensor") == 4
    local = w_query.shape[1]
    hidden = w_fc1.shape[1]
    rows = (length + 15) // 16 * 16
    pad = ((0, 0), (0, rows - length), (0, 0))
    x = jnp.pad(tokens, pad)
    g = jnp.pad(cotangent, pad)
    flat = lambda v: v.reshape(1, v.shape[0])
    full = (images, rows, width)
    thin = (images, rows, local)

    normed, query, keys, values, mixed, part = stepped(
        lambda *refs: attention_kernel(length, *refs), "attention", images,
        (x, flat(ln1_gain), flat(ln1_shift), w_query, flat(b_query), w_key, w_value,
         flat(b_value), w_proj),
        [each(full), fixed((1, width)), fixed((1, width)), fixed((width, local)),
         fixed((1, local)), fixed((width, local)), fixed((width, local)), fixed((1, local)),
         fixed((local, width))],
        [struct(full, BF16)] + [struct(thin, BF16)] * 4 + [struct(full, BF16)],
        [each(full)] + [each(thin)] * 4 + [each(full)],
        [], 2_000_000_000,
    )
    middle, resid = exchange(
        middle_kernel, 0, "middle", [struct(full, BF16), struct((rows, width), F32)], rows, width,
        [], (part, x, flat(b_proj), flat(ln2_gain), flat(ln2_shift)),
    )
    tall = (images, 2 * rows, width)
    part, fc, grad_bfc1 = stepped(
        feed_kernel, "feed", images,
        (middle, g, w_fc1, flat(b_fc1), w_fc2),
        [each(full), each(full), fixed((width, hidden)), fixed((1, hidden)),
         fixed((hidden, width))],
        [struct(tall, BF16), struct((width + hidden, width), BF16), struct((1, hidden), F32)],
        [each(tall), fixed((width + hidden, width)), fixed((1, hidden))],
        [pltpu.VMEM((width, hidden), F32), pltpu.VMEM((hidden, width), F32)], 6_000_000_000,
    )
    fc = sum_images(fc)
    both, grad_resid, small = exchange(
        turn_kernel, 1, "turn",
        [struct(tall, BF16), struct((rows, width), F32), struct((8, width), F32)],
        2 * rows, width, [],
        (part, resid, g, flat(b_fc2), flat(ln2_gain)),
    )
    layer_out = both[:, :length]
    part, gq, gk, gv, gp, bq, bv = stepped(
        lambda *refs: back_kernel(length, *refs), "back", images,
        (both, mixed, normed, query, keys, values, w_proj, w_query, w_key, w_value),
        [pl.BlockSpec((1, rows, width), lambda step: (step, 1, 0)), each(thin), each(full),
         each(thin), each(thin), each(thin), fixed((local, width))]
        + [fixed((width, local))] * 3,
        [struct(full, BF16)] + [struct((width, local), BF16)] * 3
        + [struct((local, width), BF16)] + [struct((1, local), F32)] * 2,
        [each(full)] + [fixed((width, local))] * 3 + [fixed((local, width))]
        + [fixed((1, local))] * 2,
        [pltpu.VMEM((width, local), F32)] * 3 + [pltpu.VMEM((local, width), F32)], 4_000_000_000,
    )
    heads = sum_images(
        jnp.concatenate([gq.reshape(-1, width), gk.reshape(-1, width), gv.reshape(-1, width), gp])
    )
    out, small = exchange(
        last_kernel, 2, "last", [struct(full, BF16), struct((8, width), F32)], rows, width,
        [pltpu.VMEM((2, 8, width), F32), pltpu.VMEM((2, 8, width), F32)],
        (part, x, grad_resid, flat(ln1_gain), small),
    )
    tokens_grad = out[:, :length]
    pack = jnp.concatenate(
        [small[:6].reshape(-1), grad_bfc1.reshape(-1), bq.reshape(-1), bv.reshape(-1)]
    )
    pack = sum_small(pack)
    row = lambda i: pack[i * width : (i + 1) * width]
    tail = 6 * width + hidden
    heads = heads.astype(F32)
    fc = fc.astype(F32)
    square = lambda i: heads[i * local : (i + 1) * local]
    return (
        layer_out,
        tokens_grad,
        row(4),
        row(5),
        square(0).reshape(width, local),
        pack[tail : tail + local],
        square(1).reshape(width, local),
        square(2).reshape(width, local),
        pack[tail + local : tail + 2 * local],
        square(3),
        row(2),
        row(0),
        row(1),
        fc[:width],
        pack[6 * width : tail],
        fc[width:],
        row(3),
    )


def solution(mesh):
    in_specs = (
        P("dp", None, None),
        P(),
        P(),
        P(None, "tensor"),
        P("tensor"),
        P(None, "tensor"),
        P(None, "tensor"),
        P("tensor"),
        P("tensor", None),
        P(),
        P(),
        P(),
        P(None, "tensor"),
        P("tensor"),
        P("tensor", None),
        P(),
        P("dp", None, None),
    )
    out_specs = (
        P("dp", None, None),
        P("dp", None, None),
        P(),
        P(),
        P(None, "tensor"),
        P("tensor"),
        P(None, "tensor"),
        P(None, "tensor"),
        P("tensor"),
        P("tensor", None),
        P(),
        P(),
        P(),
        P(None, "tensor"),
        P("tensor"),
        P("tensor", None),
        P(),
    )
    return jax.shard_map(shards, mesh=mesh, in_specs=in_specs, out_specs=out_specs, check_vma=False)
```

time: 537 us -> 259 us (0.48)
  blocking collectives: 165 us -> 0 us
  waiting for transfers between devices: 217 us -> 61.1 us
  Pallas kernels: 0 us -> 132 us
  matrix products: 53.8 us -> 0 us
  local copies, waits for them, and re-layouts: 55.6 us -> 37.1 us
  between operations: 15.1 us -> 1.04 us
  other arithmetic: 21.8 us -> 9.02 us
  starting transfers between devices: 6.63 us -> 18.1 us
    psum x1 -> x0, waiting for transfers between devices: 178 us -> none  [shards(): lax.psum((grad_wquery, grad_bquery, grad_wkey, grad_wvalue, grad_bvalue,...]
    pallas_call x0 -> x6, Pallas kernels: none -> 132 us  [the longest x3 95.1 us: exchange(): pl.pallas_call(kernel, out_shape=outs, in_specs=whole(len(args)), out_spe...]
    unnamed x4 -> x0, blocking collectives: 97.1 us -> none
    psum x2 -> x0, blocking collectives: 67.8 us -> none  [the longest x1 45.3 us: shards(): lax.psum((grad_ln1_gain, grad_ln1_shift, grad_bproj, grad_ln2_gain, grad_...]
    ppermute x0 -> x15, waiting for transfers between devices: none -> 61.1 us  [the longest x6 29.1 us: sum_images(): got = lax.ppermute(current, 'dp', partners(count, distance))]
    dot_general x24 -> x0, matrix products: 53.8 us -> none  [the longest x6 21.9 us: times_transpose(): lax.dot_general(left, right, (((1,), (1,)), ((), ())), preferred_element_...]
    all_gather x4 -> x0, waiting for transfers between devices: 37 us -> none  [the longest x1 20.2 us: shards(): lax.all_gather(grad_resid.astype(jnp.bfloat16), 'tensor', axis=0, tiled=T...]
    unnamed x112 -> x49, local copies, waits for them, and re-layouts: 33.1 us -> 11.7 us
  transfers between devices with their start and end apart: 9 -> 15, of which waited for: 5 -> 11; matrix products, arithmetic and copies ran while one was open for 21% -> 11% of each run, Pallas kernels for 0% -> 33%
where the time goes in v1:
time: 259 us; the launch traced here: 258 us
  Pallas kernels  132 us (51%)
  waiting for transfers between devices  61.1 us (24%)
  local copies, waits for them, and re-layouts  37.1 us (14%)
  starting transfers between devices  18.1 us (7%)
  other arithmetic  9.02 us (3%)
    pallas_call x3, Pallas kernels, exchange(): pl.pallas_call(kernel, out_shape=outs, in_specs=whole(len(args)), out_spe...  95.1 us
    pallas_call x3, Pallas kernels, stepped(): pl.pallas_call(kernel, grid=(steps,), out_shape=outs, in_specs=arg_specs,...  36.6 us
    ppermute x6, waiting for transfers between devices, sum_images(): got = lax.ppermute(current, 'dp', partners(count, distance))  29.1 us
    ppermute x6, waiting for transfers between devices, sum_images(): got = lax.ppermute(give.astype(BF16), 'dp', partners(count, distance))  27.2 us
    unnamed x49, local copies, waits for them, and re-layouts  11.7 us
    ppermute x6, starting transfers between devices, sum_images(): got = lax.ppermute(current, 'dp', partners(count, distance))  7.31 us
    ppermute x6, starting transfers between devices, sum_images(): got = lax.ppermute(give.astype(BF16), 'dp', partners(count, distance))  6.94 us
  transfers between devices with their start and end apart: 15, of which 11 were waited for; matrix products, arithmetic and copies ran while one was open for 11% of the time, Pallas kernels for 33%

profile of v1, /device:TPU:0, one launch (start us, length us, event | category | flops | bytes accessed | tf_op | source)
XLA Modules:
  0.0 258.0 jit_solution(12878395229331593923)
XLA Ops:
  0.7 1.5 copy.47
  2.3 0.6 reshape.93.refs_1_.gain
  2.8 0.6 reshape.94.refs_2_
  3.4 0.9 copy.48.refs_3_.refs_7_
  4.3 0.9 copy.49.refs_5_.refs_8_
  5.3 0.9 copy.50.refs_6_.refs_9_
  6.2 0.6 reshape.97.bias
  6.8 0.6 reshape.98.gain
  7.4 0.6 reshape.99.shift
  8.1 1.1 pad.7.refs_0_.x_ref
  9.2 1.2 pad.8.g_ref
  10.4 0.6 reshape.100.b1
  10.9 9.2 %attention.1 = (bf16[4,208,768]{2,1,0:T(8,128)(2,1)}, bf16[4,208,192]{2,1,0:T(8,128)(2,1)}, bf16[4,208,192]{2,1,0:T(8,128)(2,1)}, bf16[4,208,192]{2,1,0:T(8,128)...) custom-call(bf16[4,208,768]{2,1,0:T(8,128)(2,1)} %pad.7.refs_0_.x_ref, f32[1,768]{1,0:T(1,128)} %reshape.93.refs_1_.gain, ...), custom_call_target="tpu_custom_call" | custom-call | flops 2000000000 | bytes 20000000 | tf_op jit(solution)/shard_map/attention/pallas_call | solution.py:300
  20.1 26.3 %middle.1 = (bf16[4,208,768]{2,1,0:T(8,128)(2,1)}, f32[208,768]{1,0:T(8,128)}) custom-call(bf16[4,208,768]{2,1,0:T(8,128)(2,1)} %get-tuple-element.40.part, bf16[4,208,768]{2,1,0:T(8,128)(2,1)} %pad.7.refs_0_.x_ref, f32[1,768]{1,0:T(1,128)} %reshape.97.bias, f32[1,768]{1,0:T(1,128)} %reshape.98.gain, f32[1,768]{1,0:T(1,128)} %reshape.99.shift), custom_call_target="tpu_custom_call" | custom-call | bytes 50000000 | tf_op jit(solution)/shard_map/middle/pallas_call | solution.py:277
  46.4 12.2 %feed.1 = (bf16[4,416,768]{2,1,0:T(8,128)(2,1)}, bf16[1536,768]{1,0:T(8,128)(2,1)}, f32[1,768]{1,0:T(1,128)}) custom-call(bf16[4,208,768]{2,1,0:T(8,128)(2,1)} %get-tuple-element.41.c_ref, bf16[4,208,768]{2,1,0:T(8,128)(2,1)} %pad.8.g_ref, bf16[768,768]{1,0:T(8,128)(2,1)} %w1.1, f32[1,768]{1,0:T(1,128)} %reshape.100.b1, bf16[768,768]{1,0:T(8,128)(2,1)} %w2.1), custom_call_target="tpu_custom_call" | custom-call | flops 6000000000 | bytes 20000000 | tf_op jit(solution)/shard_map/feed/pallas_call | solution.py:300
  58.6 1.4 constant_dynamic-slice_fusion
  60.0 1.6 collective-permute-start.9
  61.6 0.6 reshape.101.bias
  62.2 41.0 %turn.1 = (bf16[4,416,768]{2,1,0:T(8,128)(2,1)}, f32[208,768]{1,0:T(8,128)}, f32[8,768]{1,0:T(8,128)}) custom-call(bf16[4,416,768]{2,1,0:T(8,128)(2,1)} %get-tuple-element.42.part, f32[208,768]{1,0:T(8,128)} %get-tuple-element.43.h_ref, bf16[4,208,768]{2,1,0:T(8,128)(2,1)} %pad.8.g_ref, f32[1,768]{1,0:T(1,128)} %reshape.101.bias, f32[1,768]{1,0:T(1,128)} %reshape.98.gain), custom_call_target="tpu_custom_call" | custom-call | bytes 50000000 | tf_op jit(solution)/shard_map/turn/pallas_call | solution.py:277
  103.2 15.3 %back.1 = (bf16[4,208,768]{2,1,0:T(8,128)(2,1)}, bf16[768,192]{1,0:T(8,128)(2,1)}, bf16[768,192]{1,0:T(8,128)(2,1)}, bf16[768,192]{1,0:T(8,128)(2,1)}, bf16[192,...) custom-call(bf16[4,416,768]{2,1,0:T(8,128)(2,1)} %get-tuple-element.44.refs_0_, ...), custom_call_target="tpu_custom_call" | custom-call | flops 4000000000 | bytes 20000000 | tf_op jit(solution)/shard_map/back/pallas_call | solution.py:300
  118.5 1.4 reshape.106
  119.9 2.1 reshape.107
  122.0 1.9 convert_add_fusion
  123.9 0.9 dynamic-slice_convert_fusion
  124.8 1.6 collective-permute-start.10
  126.4 2.1 reshape.108
  128.5 1.0 constant_dynamic-update-slice_fusion.1
  129.5 1.0 constant_dynamic-update-slice_fusion
  130.4 0.9 constant_dynamic-slice_fusion.1
  131.9 8.8 %collective-permute-done.10 = bf16[384,768]{1,0:T(8,128)(2,1)} collective-permute-done((bf16[384,768]{1,0:T(8,128)(2,1)}, bf16[384,768]{1,0:T(8,128)(2,1)}, u32[]{:S(2)}, u32[]{:S(2)}) %collective-permute-start.10) | collective-permute-done | bytes 589856 | tf_op jit(solution)/shard_map/ppermute | solution.py:333
  140.7 1.3 convert_add_fusion.1
  142.0 2.6 %collective-permute-start.11 = (bf16[192,768]{1,0:T(8,128)(2,1)S(1)}, bf16[192,768]{1,0:T(8,128)(2,1)S(1)}, u32[]{:S(2)}, u32[]{:S(2)}) collective-permute-start(bf16[192,768]{1,0:T(8,128)(2,1)S(1)} %dynamic-slice_convert_fusion.1), channel_id=1, source_target_pairs={{0,16},{4,20},{8,24},{12,28},{16,0},{20,4},{24,8},{28,12},{1,17},{... | collective-permute-start | bytes 884744 | tf_op jit(solution)/shard_map/ppermute | solution.py:333
  144.6 2.4 collective-permute-done.3
  147.0 1.2 convert_add_fusion.2
  148.2 0.5 collective-permute-start.4
  148.8 9.1 %collective-permute-done.11 = bf16[192,768]{1,0:T(8,128)(2,1)S(1)} collective-permute-done((bf16[192,768]{1,0:T(8,128)(2,1)S(1)}, bf16[192,768]{1,0:T(8,128)(2,1)S(1)}, u32[]{:S(2)}, u32[]{:S(2)}) %collective-permute-start.11) | collective-permute-done | bytes 294944 | tf_op jit(solution)/shard_map/ppermute | solution.py:333
  158.0 5.6 %collective-permute-done.4 = bf16[192,768]{1,0:T(8,128)(2,1)S(1)} collective-permute-done((bf16[192,768]{1,0:T(8,128)(2,1)S(1)}, bf16[192,768]{1,0:T(8,128)(2,1)S(1)}, u32[]{:S(2)}, u32[]{:S(2)}) %collective-permute-start.4) | collective-permute-done | bytes 294944 | tf_op jit(solution)/shard_map/ppermute | solution.py:333
  163.8 14.0 %collective-permute-done.12 = bf16[192,768]{1,0:T(8,128)(2,1)S(1)} collective-permute-done((bf16[192,768]{1,0:T(8,128)(2,1)S(1)}, bf16[192,768]{1,0:T(8,128)(2,1)S(1)}, u32[]{:S(2)}, u32[]{:S(2)}) %collective-permute-start.12) | collective-permute-done | bytes 294944 | tf_op jit(solution)/shard_map/ppermute | solution.py:338
  178.1 1.4 collective-permute-done.5
  179.6 11.2 %collective-permute-done.6 = bf16[96,768]{1,0:T(8,128)(2,1)S(1)} collective-permute-done((bf16[96,768]{1,0:T(8,128)(2,1)S(1)}, bf16[96,768]{1,0:T(8,128)(2,1)S(1)}, u32[]{:S(2)}, u32[]{:S(2)}) %collective-permute-start.6) | collective-permute-done | bytes 147488 | tf_op jit(solution)/shard_map/ppermute | solution.py:338
  190.8 5.6 %collective-permute-start.7 = (bf16[192,768]{1,0:T(8,128)(2,1)S(1)}, bf16[192,768]{1,0:T(8,128)(2,1)S(1)}, u32[]{:S(2)}, u32[]{:S(2)}) collective-permute-start(bf16[192,768]{1,0:T(8,128)(2,1)S(1)} %maximum_select_fusion.5), channel_id=1, source_target_pairs={{0,8},{4,12},{8,0},{12,4},{16,24},{20,28},{24,16},{28,20},{1,9},{5... | collective-permute-start | bytes 884744 | tf_op jit(solution)/shard_map/ppermute | solution.py:338
  197.3 0.7 collective-permute-start.14
  198.0 3.5 %collective-permute-done.7 = bf16[192,768]{1,0:T(8,128)(2,1)S(1)} collective-permute-done((bf16[192,768]{1,0:T(8,128)(2,1)S(1)}, bf16[192,768]{1,0:T(8,128)(2,1)S(1)}, u32[]{:S(2)}, u32[]{:S(2)}) %collective-permute-start.7) | collective-permute-done | bytes 294944 | tf_op jit(solution)/shard_map/ppermute | solution.py:338
  201.7 0.7 collective-permute-start.8
  202.4 27.7 %last.1 = (bf16[4,208,768]{2,1,0:T(8,128)(2,1)}, f32[8,768]{1,0:T(8,128)}) custom-call(bf16[4,208,768]{2,1,0:T(8,128)(2,1)} %get-tuple-element.50.part, bf16[4,208,768]{2,1,0:T(8,128)(2,1)} %pad.7.refs_0_.x_ref, f32[208,768]{1,0:T(8,128)} %get-tuple-element.51.dh_ref, f32[1,768]{1,0:T(1,128)} %reshape.93.refs_1_.gain, f32[8,768]{1,0:T(8,128)} %get-tuple-element.52.small_in), custom_call_target="tpu_custom_call" | custom-call | bytes 50000000 | tf_op jit(solution)/shard_map/last/pallas_call | solution.py:277
  230.2 0.7 reshape.102
  231.0 1.6 collective-permute-start
  232.6 2.4 collective-permute-done
  235.0 1.5 collective-permute-start.1
  236.5 2.3 collective-permute-done.1
  238.8 0.8 collective-permute-start.2
  239.6 1.4 slice.54
  241.0 1.5 copy.55
  242.6 1.5 copy.56
  244.1 0.6 fusion.5
  244.7 0.6 fusion.4
  245.3 1.5 fusion.1
  246.9 1.2 fusion.3
  248.1 1.4 reshape.109
  249.5 1.1 copy.57
  250.9 1.1 copy.58
  252.3 1.1 copy.59
  253.3 2.1 fusion
  255.5 2.5 fusion.2
  (67 shorter events, 3.4 us)
Async XLA Ops:
  0.7 1.5 copy-start.8
  0.7 2.2 copy-start.9
  0.7 2.7 %copy-start.5 = (bf16[768,192]{0,1:T(8,128)(2,1)S(1)}, bf16[768,192]{0,1:T(8,128)(2,1)}, u32[]{:S(2)}) copy-start(bf16[768,192]{0,1:T(8,128)(2,1)} %param.20) | copy-start | bytes 884740
  0.7 3.7 %copy-start.6 = (bf16[768,192]{0,1:T(8,128)(2,1)S(1)}, bf16[768,192]{0,1:T(8,128)(2,1)}, u32[]{:S(2)}) copy-start(bf16[768,192]{0,1:T(8,128)(2,1)} %param.22) | copy-start | bytes 884740
  0.7 4.6 %copy-start.7 = (bf16[768,192]{0,1:T(8,128)(2,1)S(1)}, bf16[768,192]{0,1:T(8,128)(2,1)}, u32[]{:S(2)}) copy-start(bf16[768,192]{0,1:T(8,128)(2,1)} %param.23) | copy-start | bytes 884740
  2.2 4.0 %copy-start.10 = (f32[768]{0:T(1024)S(1)}, f32[768]{0:T(1024)}, u32[]{:S(2)}) copy-start(f32[768]{0:T(1024)} %param.26) | copy-start | bytes 9220
  2.2 4.6 %copy-start.11 = (f32[768]{0:T(1024)S(1)}, f32[768]{0:T(1024)}, u32[]{:S(2)}) copy-start(f32[768]{0:T(1024)} %param.27) | copy-start | bytes 9220
  2.2 5.1 %copy-start.12 = (f32[768]{0:T(1024)S(1)}, f32[768]{0:T(1024)}, u32[]{:S(2)}) copy-start(f32[768]{0:T(1024)} %param.28) | copy-start | bytes 9220
  2.2 5.7 %copy-start.2 = (bf16[4,197,768]{2,0,1:T(4,128)(2,1)S(1)}, bf16[4,197,768]{2,0,1:T(4,128)(2,1)}, u32[]{:S(2)}) copy-start(bf16[4,197,768]{2,0,1:T(4,128)(2,1)} %param.33) | copy-start | bytes 3631108
  9.2 1.2 copy-start.13
  58.6 3.0 %copy-start.14 = (f32[768]{0:T(1024)S(1)}, f32[768]{0:T(1024)}, u32[]{:S(2)}) copy-start(f32[768]{0:T(1024)} %param.32) | copy-start | bytes 9220
  60.0 62.0 %collective-permute-start.9 = (bf16[768,768]{1,0:T(8,128)(2,1)S(1)}, bf16[768,768]{1,0:T(8,128)(2,1)}, u32[]{:S(2)}, u32[]{:S(2)}) collective-permute-start(bf16[768,768]{1,0:T(8,128)(2,1)S(1)} %constant_dynamic-slice_fusion), channel_id=1, source_target_pairs={{0,4},{4,0},{8,12},{12,8},{16,20},{20,16},{24,28},{28,24},{1,5},{5... | collective-permute-start | bytes 3538952 | tf_op jit(solution)/shard_map/ppermute | solution.py:333
  123.9 2.5 copy-start.4
  124.8 15.9 %collective-permute-start.10 = (bf16[384,768]{1,0:T(8,128)(2,1)}, bf16[384,768]{1,0:T(8,128)(2,1)}, u32[]{:S(2)}, u32[]{:S(2)}) collective-permute-start(bf16[384,768]{1,0:T(8,128)(2,1)} %dynamic-slice_convert_fusion), channel_id=1, source_target_pairs={{0,8},{4,12},{8,0},{12,4},{16,24},{20,28},{24,16},{28,20},{1,9},{5... | collective-permute-start | bytes 1769480 | tf_op jit(solution)/shard_map/ppermute | solution.py:333
  130.4 1.5 copy-start
  131.4 15.6 %collective-permute-start.3 = (bf16[384,768]{1,0:T(8,128)(2,1)}, bf16[384,768]{1,0:T(8,128)(2,1)}, u32[]{:S(2)}, u32[]{:S(2)}) collective-permute-start(bf16[384,768]{1,0:T(8,128)(2,1)} %constant_dynamic-slice_fusion.1), channel_id=1, source_target_pairs={{0,4},{4,0},{8,12},{12,8},{16,20},{20,16},{24,28},{28,24},{1,5},{5... | collective-permute-start | bytes 1769480 | tf_op jit(solution)/shard_map/ppermute | solution.py:333
  140.7 6.3 %copy-start.1 = (bf16[768,768]{1,0:T(8,128)(2,1)S(1)}, bf16[768,768]{1,0:T(8,128)(2,1)}, u32[]{:S(2)}) copy-start(bf16[768,768]{1,0:T(8,128)(2,1)} %copy-done) | copy-start | bytes 3538948
  142.0 15.9 %collective-permute-start.11 = (bf16[192,768]{1,0:T(8,128)(2,1)S(1)}, bf16[192,768]{1,0:T(8,128)(2,1)S(1)}, u32[]{:S(2)}, u32[]{:S(2)}) collective-permute-start(bf16[192,768]{1,0:T(8,128)(2,1)S(1)} %dynamic-slice_convert_fusion.1), channel_id=1, source_target_pairs={{0,16},{4,20},{8,24},{12,28},{16,0},{20,4},{24,8},{28,12},{1,17},{... | collective-permute-start | bytes 884744 | tf_op jit(solution)/shard_map/ppermute | solution.py:333
  148.2 15.4 %collective-permute-start.4 = (bf16[192,768]{1,0:T(8,128)(2,1)S(1)}, bf16[192,768]{1,0:T(8,128)(2,1)S(1)}, u32[]{:S(2)}, u32[]{:S(2)}) collective-permute-start(bf16[192,768]{1,0:T(8,128)(2,1)S(1)} %dynamic-slice_convert_fusion.2), channel_id=1, source_target_pairs={{0,8},{4,12},{8,0},{12,4},{16,24},{20,28},{24,16},{28,20},{1,9},{5... | collective-permute-start | bytes 884744 | tf_op jit(solution)/shard_map/ppermute | solution.py:333
  157.9 19.9 %collective-permute-start.12 = (bf16[192,768]{1,0:T(8,128)(2,1)S(1)}, bf16[192,768]{1,0:T(8,128)(2,1)S(1)}, u32[]{:S(2)}, u32[]{:S(2)}) collective-permute-start(bf16[192,768]{1,0:T(8,128)(2,1)S(1)} %add_convert_fusion), channel_id=1, source_target_pairs={{0,16},{4,20},{8,24},{12,28},{16,0},{20,4},{24,8},{28,12},{1,17},{... | collective-permute-start | bytes 884744 | tf_op jit(solution)/shard_map/ppermute | solution.py:338
  163.7 15.8 %collective-permute-start.5 = (bf16[96,768]{1,0:T(8,128)(2,1)S(1)}, bf16[96,768]{1,0:T(8,128)(2,1)S(1)}, u32[]{:S(2)}, u32[]{:S(2)}) collective-permute-start(bf16[96,768]{1,0:T(8,128)(2,1)S(1)} %dynamic-slice_convert_fusion.3), channel_id=1, source_target_pairs={{0,16},{4,20},{8,24},{12,28},{16,0},{20,4},{24,8},{28,12},{1,17},{... | collective-permute-start | bytes 442376 | tf_op jit(solution)/shard_map/ppermute | solution.py:333
  178.0 18.8 %collective-permute-start.13 = (bf16[384,768]{1,0:T(8,128)(2,1)S(1)}, bf16[384,768]{1,0:T(8,128)(2,1)S(1)}, u32[]{:S(2)}, u32[]{:S(2)}) collective-permute-start(bf16[384,768]{1,0:T(8,128)(2,1)S(1)} %maximum_select_fusion.4), channel_id=1, source_target_pairs={{0,8},{4,12},{8,0},{12,4},{16,24},{20,28},{24,16},{28,20},{1,9},{5... | collective-permute-start | bytes 1769480 | tf_op jit(solution)/shard_map/ppermute | solution.py:338
  179.5 11.2 %collective-permute-start.6 = (bf16[96,768]{1,0:T(8,128)(2,1)S(1)}, bf16[96,768]{1,0:T(8,128)(2,1)S(1)}, u32[]{:S(2)}, u32[]{:S(2)}) collective-permute-start(bf16[96,768]{1,0:T(8,128)(2,1)S(1)} %add_convert_fusion.1), channel_id=1, source_target_pairs={{0,16},{4,20},{8,24},{12,28},{16,0},{20,4},{24,8},{28,12},{1,17},{... | collective-permute-start | bytes 442376 | tf_op jit(solution)/shard_map/ppermute | solution.py:338
  190.8 10.7 %collective-permute-start.7 = (bf16[192,768]{1,0:T(8,128)(2,1)S(1)}, bf16[192,768]{1,0:T(8,128)(2,1)S(1)}, u32[]{:S(2)}, u32[]{:S(2)}) collective-permute-start(bf16[192,768]{1,0:T(8,128)(2,1)S(1)} %maximum_select_fusion.5), channel_id=1, source_target_pairs={{0,8},{4,12},{8,0},{12,4},{16,24},{20,28},{24,16},{28,20},{1,9},{5... | collective-permute-start | bytes 884744 | tf_op jit(solution)/shard_map/ppermute | solution.py:338
  197.3 56.0 %collective-permute-start.14 = (bf16[768,768]{1,0:T(8,128)(2,1)S(1)}, bf16[768,768]{1,0:T(8,128)(2,1)}, u32[]{:S(2)}, u32[]{:S(2)}) collective-permute-start(bf16[768,768]{1,0:T(8,128)(2,1)S(1)} %maximum_select_fusion.2), channel_id=1, source_target_pairs={{0,4},{4,0},{8,12},{12,8},{16,20},{20,16},{24,28},{28,24},{1,5},{5... | collective-permute-start | bytes 3538952 | tf_op jit(solution)/shard_map/ppermute | solution.py:338
  201.7 43.7 %collective-permute-start.8 = (bf16[384,768]{1,0:T(8,128)(2,1)S(1)}, bf16[384,768]{1,0:T(8,128)(2,1)}, u32[]{:S(2)}, u32[]{:S(2)}) collective-permute-start(bf16[384,768]{1,0:T(8,128)(2,1)S(1)} %maximum_select_fusion.3), channel_id=1, source_target_pairs={{0,4},{4,0},{8,12},{12,8},{16,20},{20,16},{24,28},{28,24},{1,5},{5... | collective-permute-start | bytes 1769480 | tf_op jit(solution)/shard_map/ppermute | solution.py:338
  202.4 28.5 %copy-start.15 = (f32[1,768]{1,0:T(1,128)S(1)}, f32[1,768]{1,0:T(1,128)}, u32[]{:S(2)}) copy-start(f32[1,768]{1,0:T(1,128)} %get-tuple-element.55) | copy-start | bytes 9220
  202.4 28.5 %copy-start.16 = (f32[1,192]{1,0:T(1,128)S(1)}, f32[1,192]{1,0:T(1,128)}, u32[]{:S(2)}) copy-start(f32[1,192]{1,0:T(1,128)} %get-tuple-element.56) | copy-start | bytes 2308
  202.4 28.5 %copy-start.17 = (f32[1,192]{1,0:T(1,128)S(1)}, f32[1,192]{1,0:T(1,128)}, u32[]{:S(2)}) copy-start(f32[1,192]{1,0:T(1,128)} %get-tuple-element.57) | copy-start | bytes 2308
  231.0 4.0 %collective-permute-start = (f32[5760]{0:T(1024)S(1)}, f32[5760]{0:T(1024)S(1)}, u32[]{:S(2)}, u32[]{:S(2)}) collective-permute-start(f32[5760]{0:T(1024)S(1)} %concatenate.42), channel_id=1, source_target_pairs={{0,4},{4,0},{8,12},{12,8},{16,20},{20,16},{24,28},{28,24},{1,5},{5... | collective-permute-start | bytes 69128 | tf_op jit(solution)/shard_map/ppermute | solution.py:351
  235.0 3.8 %collective-permute-start.1 = (f32[5760]{0:T(1024)S(1)}, f32[5760]{0:T(1024)S(1)}, u32[]{:S(2)}, u32[]{:S(2)}) collective-permute-start(f32[5760]{0:T(1024)S(1)} %add.89), channel_id=1, source_target_pairs={{0,8},{4,12},{8,0},{12,4},{16,24},{20,28},{24,16},{28,20},{1,9},{5... | collective-permute-start | bytes 69128 | tf_op jit(solution)/shard_map/ppermute | solution.py:351
  238.8 5.2 %collective-permute-start.2 = (f32[5760]{0:T(1024)S(1)}, f32[5760]{0:T(1024)S(1)}, u32[]{:S(2)}, u32[]{:S(2)}) collective-permute-start(f32[5760]{0:T(1024)S(1)} %add.90), channel_id=1, source_target_pairs={{0,16},{4,20},{8,24},{12,28},{16,0},{20,4},{24,8},{28,12},{1,17},{... | collective-permute-start | bytes 69128 | tf_op jit(solution)/shard_map/ppermute | solution.py:351
  241.0 1.5 copy-start.3

commit v2 on v1

v2 whole, which is shorter than its diff:
```python
import jax
import jax.numpy as jnp
from jax import lax
from jax.experimental import pallas as pl
from jax.experimental.pallas import tpu as pltpu
from jax.sharding import PartitionSpec as P

HEAD_DIM = 64
EPSILON = 1e-06
BF16 = jnp.bfloat16
F32 = jnp.float32
MESH = pl.DeviceIdType.MESH
VMEM_LIMIT = 56 * 1024 * 1024


def matmul(left, right):
    return jnp.dot(left, right, preferred_element_type=F32)


def inner_rows(left, right):
    return lax.dot_general(left, right, (((0,), (0,)), ((), ())), preferred_element_type=F32)


def times_transpose(left, right):
    return lax.dot_general(left, right, (((1,), (1,)), ((), ())), preferred_element_type=F32)


def normalize(values):
    center = values - jnp.mean(values, axis=-1, keepdims=True)
    scale = lax.rsqrt(jnp.mean(center * center, axis=-1, keepdims=True) + EPSILON)
    return center * scale, scale


def norm_back(hat, scale, gain, grad):
    inner = grad * gain
    return scale * (
        inner
        - jnp.mean(inner, axis=-1, keepdims=True)
        - hat * jnp.mean(inner * hat, axis=-1, keepdims=True)
    )


def soft_probs(query, keys, length):
    scores = times_transpose(query, keys) * (HEAD_DIM**-0.5)
    column = lax.broadcasted_iota(jnp.int32, scores.shape, 1)
    scores = jnp.where(column < length, scores, -1e30)
    raised = jnp.exp(scores - jnp.max(scores, axis=-1, keepdims=True))
    return raised * (1.0 / jnp.sum(raised, axis=-1, keepdims=True))


def attention_kernel(
    length, x_ref, vec, bias, wq, wk, wv, wp, a_ref, q_ref, k_ref, v_ref, o_ref, part_ref
):
    hat, _ = normalize(x_ref[0].astype(F32))
    normed = (hat * vec[0:1] + vec[1:2]).astype(BF16)
    a_ref[0] = normed
    query = (matmul(normed, wq[...]) + bias[0:1]).astype(BF16)
    keys = matmul(normed, wk[...]).astype(BF16)
    values = (matmul(normed, wv[...]) + bias[1:2]).astype(BF16)
    q_ref[0] = query
    k_ref[0] = keys
    v_ref[0] = values
    heads = []
    for head in range(query.shape[1] // HEAD_DIM):
        cols = slice(head * HEAD_DIM, (head + 1) * HEAD_DIM)
        probs = soft_probs(query[:, cols], keys[:, cols], length)
        heads.append(matmul(probs.astype(BF16), values[:, cols]))
    mixed = jnp.concatenate(heads, axis=1).astype(BF16)
    o_ref[0] = mixed
    part_ref[0] = matmul(mixed, wp[...]).astype(BF16)


def feed_kernel(c_ref, g_ref, w1, vec, w2, part_ref, fc_ref, bias_ref, acc1, acc2):
    step = pl.program_id(0)
    rows = c_ref.shape[1]
    width = c_ref.shape[2]

    @pl.when(step == 0)
    def _():
        acc1[...] = jnp.zeros_like(acc1)
        acc2[...] = jnp.zeros_like(acc2)
        bias_ref[...] = jnp.zeros_like(bias_ref)

    middle = c_ref[0]
    grad = g_ref[0]
    hidden = matmul(middle, w1[...]) + vec[6:7]
    cdf = 0.5 * (1.0 + lax.erf(hidden * (0.5**0.5)))
    slope = cdf + hidden * jnp.exp(-0.5 * hidden * hidden) * 0.3989422804014327
    active = (hidden * cdf).astype(BF16)
    grad_hidden = (times_transpose(grad, w2[...]) * slope).astype(BF16)
    part_ref[0, :rows] = matmul(active, w2[...]).astype(BF16)
    part_ref[0, rows:] = times_transpose(grad_hidden, w1[...]).astype(BF16)
    acc2[...] += inner_rows(active, grad)
    acc1[...] += inner_rows(middle, grad_hidden)
    bias_ref[...] += jnp.sum(grad_hidden.astype(F32), axis=0, keepdims=True)

    @pl.when(step == pl.num_programs(0) - 1)
    def _():
        fc_ref[:width] = acc1[...].astype(BF16)
        fc_ref[width:] = acc2[...].astype(BF16)


def back_kernel(
    length, h_ref, o_ref, a_ref, q_ref, k_ref, v_ref, wp, wq, wk, wv,
    part_ref, grads_ref, bias_ref, acc,
):
    step = pl.program_id(0)

    @pl.when(step == 0)
    def _():
        acc[...] = jnp.zeros_like(acc)
        bias_ref[...] = jnp.zeros_like(bias_ref)

    low = h_ref[0]
    acc[3] += inner_rows(o_ref[0], low)
    grad_mixed = times_transpose(low, wp[...]).astype(BF16)
    normed = a_ref[0]
    query, keys, values = q_ref[0], k_ref[0], v_ref[0]
    score_scale = HEAD_DIM**-0.5
    dq, dk, dv = [], [], []
    for head in range(query.shape[1] // HEAD_DIM):
        cols = slice(head * HEAD_DIM, (head + 1) * HEAD_DIM)
        qh, kh, vh, gh = query[:, cols], keys[:, cols], values[:, cols], grad_mixed[:, cols]
        probs = soft_probs(qh, kh, length)
        dv.append(inner_rows(probs.astype(BF16), gh))
        grad_probs = times_transpose(gh, vh)
        total = jnp.sum(probs * grad_probs, axis=-1, keepdims=True)
        grad_scores = (probs * (grad_probs - total)).astype(BF16)
        dq.append(matmul(grad_scores, kh) * score_scale)
        dk.append(inner_rows(grad_scores, qh) * score_scale)
    dq = jnp.concatenate(dq, axis=1).astype(BF16)
    dk = jnp.concatenate(dk, axis=1).astype(BF16)
    dv = jnp.concatenate(dv, axis=1).astype(BF16)
    bias_ref[0:1] += jnp.sum(dq.astype(F32), axis=0, keepdims=True)
    bias_ref[1:2] += jnp.sum(dv.astype(F32), axis=0, keepdims=True)
    part_ref[0] = (
        times_transpose(dq, wq[...]) + times_transpose(dk, wk[...]) + times_transpose(dv, wv[...])
    ).astype(BF16)
    acc[0] += inner_rows(dq, normed)
    acc[1] += inner_rows(dk, normed)
    acc[2] += inner_rows(dv, normed)

    @pl.when(step == pl.num_programs(0) - 1)
    def _():
        local = acc.shape[1]
        for index in range(4):
            grads_ref[index * local : (index + 1) * local] = acc[index].astype(BF16)


def places():
    here = lax.axis_index("tensor")
    return here, here + 1 - 2 * (here % 2), (here + 2) % 4, 3 - here


def mirror(distance):
    me = lax.axis_index("dp")
    return me + distance - 2 * distance * ((me // distance) % 2)


def greet(others):
    barrier = pltpu.get_barrier_semaphore()
    for other in others:
        pl.semaphore_signal(barrier, inc=1, device_id=other, device_id_type=MESH)
    pl.semaphore_wait(barrier, len(others))


class Sender:
    def __init__(self, sems):
        self.sems = sems
        self.used = 0

    def __call__(self, src, dst, other):
        copy = pltpu.make_async_remote_copy(
            src_ref=src,
            dst_ref=dst,
            send_sem=self.sems.at[0, self.used],
            recv_sem=self.sems.at[1, self.used],
            device_id=other,
            device_id_type=MESH,
        )
        self.used += 1
        copy.start()
        return copy


def take_turns(tasks):
    tasks = list(tasks)
    while tasks:
        for task in list(tasks):
            try:
                next(task)
            except StopIteration:
                tasks.remove(task)


def halvings(first, size, distances):
    steps = []
    offset = first
    for distance in distances:
        half = size // 2
        if half % 16 == 0:
            bit = (lax.axis_index("dp") // distance) % 2
            steps.append((distance, offset + bit * half, offset + (1 - bit) * half, half, True))
            offset = offset + bit * half
            size = half
        else:
            steps.append((distance, offset, offset, size, False))
    return steps


def span(offset, rows):
    return pl.ds(pl.multiple_of(offset, 16), rows)


def sum_down(send, source, work, landing, first, steps):
    at = first
    for distance, kept, given, rows, _ in steps:
        slot = pl.ds(at, rows)
        copy = send(source.at[span(given, rows)], landing.at[slot], {"dp": mirror(distance)})
        yield
        copy.wait()
        mine = source[span(kept, rows)].astype(F32)
        work[span(kept, rows)] = (mine + landing[slot].astype(F32)).astype(BF16)
        source = work
        at += rows


def spread_up(send, work, steps):
    for distance, kept, _, rows, halved in reversed(steps):
        if halved:
            region = work.at[span(kept, rows)]
            copy = send(region, region, {"dp": mirror(distance)})
            yield
            copy.wait()


def sum_all(send, source, work, result, landing, first, steps):
    yield from sum_down(send, source, work, landing, first, steps)
    _, kept, _, rows, _ = steps[-1]
    result[span(kept, rows)] = work[span(kept, rows)]
    yield from spread_up(send, result, steps)


def landing_rows(size, distances):
    return sum(rows for _, _, _, rows, _ in halvings(0, size, distances))


def reduce_share(send, part, near_in, out_buf, far_in):
    here, near, far, diag = places()
    first = send(part.at[diag], near_in.at[0], {"tensor": near})
    second = send(part.at[near], near_in.at[1], {"tensor": near})
    yield
    first.wait_recv()
    out_buf[...] = (part[far].astype(F32) + near_in[0].astype(F32)).astype(BF16)
    third = send(out_buf, far_in, {"tensor": far})
    yield
    second.wait_recv()
    near_sum = part[here].astype(F32) + near_in[1].astype(F32)
    third.wait_recv()
    total = near_sum + far_in[...].astype(F32)
    first.wait_send()
    second.wait_send()
    third.wait_send()
    return total


def gather_share(send, out):
    here, near, far, diag = places()
    first = send(out.at[here], out.at[here], {"tensor": far})
    second = send(out.at[here], out.at[here], {"tensor": near})
    yield
    first.wait_recv()
    third = send(out.at[far], out.at[far], {"tensor": near})
    yield
    second.wait_recv()
    third.wait_recv()
    first.wait_send()
    second.wait_send()
    third.wait_send()


def tensor_others():
    _, near, far, _ = places()
    return [{"tensor": near}, {"tensor": far}]


def dp_orders(count):
    distances = [1 << i for i in range(count.bit_length() - 1)]
    return distances, distances[1:] + distances[:1]


def middle_kernel(part, x_ref, vec, out, h_ref, near_in, out_buf, far_in, sems):
    here, near, far, _ = places()
    send = Sender(sems)
    greet(tensor_others())

    def task():
        total = yield from reduce_share(send, part, near_in, out_buf, far_in)
        resid = x_ref[here].astype(F32) + total + vec[2:3]
        h_ref[...] = resid
        hat, _ = normalize(resid)
        out[here] = (hat * vec[3:4] + vec[4:5]).astype(BF16)
        yield from gather_share(send, out)

    take_turns([task()])


def turn_kernel(
    count, part, h_ref, g_ref, vec, fc, out, dh_ref, small, work,
    near_in, out_buf, far_in, sems, landing,
):
    here = lax.axis_index("tensor")
    rows = h_ref.shape[0]
    send = Sender(sems)
    one, two = dp_orders(count)
    greet(tensor_others() + [{"dp": mirror(d)} for d in one])
    half = fc.shape[0] // 2

    def task():
        total = yield from reduce_share(send, part, near_in, out_buf, far_in)
        resid = h_ref[...]
        grad = total[rows:]
        own = g_ref[here].astype(F32)
        hat, scale = normalize(resid)
        grad_resid = own + norm_back(hat, scale, vec[3:4], grad)
        dh_ref[...] = grad_resid
        out[here, :rows] = (resid + total[:rows] + vec[5:6]).astype(BF16)
        out[here, rows:] = grad_resid.astype(BF16)
        small[0:1] = jnp.sum(grad * hat, axis=0, keepdims=True)
        small[1:2] = jnp.sum(grad, axis=0, keepdims=True)
        small[2:3] = jnp.sum(grad_resid, axis=0, keepdims=True)
        small[3:4] = jnp.sum(own, axis=0, keepdims=True)
        small[4:8] = jnp.zeros((4, small.shape[1]), F32)
        yield from gather_share(send, out)

    take_turns([
        task(),
        sum_down(send, fc, work, landing, 0, halvings(0, half, one)),
        sum_down(send, fc, work, landing, landing_rows(half, one), halvings(half, half, two)),
    ])


def last_kernel(
    count, part, x_ref, dh_ref, vec, small_in, bfc1, bqv, fc, heads,
    out, small, fc_out, heads_out,
    near_in, out_buf, far_in, sems, work, landing, sums, got,
):
    here, near, far, _ = places()
    send = Sender(sems)
    one, two = dp_orders(count)
    greet(tensor_others() + [{"dp": mirror(d)} for d in one])
    fc_half = fc.shape[0] // 2
    half = heads.shape[0] // 2
    local = bqv.shape[1]
    fc_steps = halvings(0, fc_half, one), halvings(fc_half, fc_half, two)
    for steps in fc_steps:
        _, kept, _, rows, _ = steps[-1]
        fc_out[span(kept, rows)] = fc[span(kept, rows)]

    def task():
        total = yield from reduce_share(send, part, near_in, out_buf, far_in)
        hat, scale = normalize(x_ref[here].astype(F32))
        out[here] = (dh_ref[...] + norm_back(hat, scale, vec[0:1], total)).astype(BF16)
        sums[0, :8] = small_in[...]
        sums[0, 4:5] = jnp.sum(total * hat, axis=0, keepdims=True)
        sums[0, 5:6] = jnp.sum(total, axis=0, keepdims=True)
        copy = send(sums.at[0], got.at[0], {"tensor": near})
        yield from gather_share(send, out)
        copy.wait()
        sums[1] = sums[0] + got[0]
        copy = send(sums.at[1], got.at[1], {"tensor": far})
        yield
        copy.wait()
        sums[2] = sums[1] + got[1]
        sums[2, 8:9] = bfc1[...]
        sums[2, 9:11, :local] = bqv[...]
        for slot, distance in enumerate(one, 2):
            copy = send(sums.at[slot], got.at[slot], {"dp": mirror(distance)})
            yield
            copy.wait()
            sums[slot + 1] = sums[slot] + got[slot]
        small[...] = sums[len(one) + 2]

    sums[0, 8:16] = jnp.zeros((8, sums.shape[2]), F32)
    take_turns([
        task(),
        spread_up(send, fc_out, fc_steps[0]),
        spread_up(send, fc_out, fc_steps[1]),
        sum_all(send, heads, work, heads_out, landing, 0, halvings(0, half, one)),
        sum_all(
            send, heads, work, heads_out, landing, landing_rows(half, one),
            halvings(half, half, two),
        ),
    ])


def whole(count):
    return [pl.BlockSpec(memory_space=pltpu.VMEM)] * count


def fixed(shape):
    return pl.BlockSpec(shape, lambda step: (0,) * len(shape))


def each(shape):
    return pl.BlockSpec((1,) + shape[1:], lambda step: (step,) + (0,) * (len(shape) - 1))


def struct(shape, dtype):
    return jax.ShapeDtypeStruct(shape, dtype)


def exchange(kernel, number, name, outs, rows, width, extra, args):
    return pl.pallas_call(
        kernel,
        out_shape=outs,
        in_specs=whole(len(args)),
        out_specs=whole(len(outs)),
        scratch_shapes=[
            pltpu.VMEM((2, rows, width), BF16),
            pltpu.VMEM((rows, width), BF16),
            pltpu.VMEM((rows, width), BF16),
            pltpu.SemaphoreType.DMA((2, 64)),
            *extra,
        ],
        compiler_params=pltpu.CompilerParams(
            collective_id=number, has_side_effects=True, vmem_limit_bytes=VMEM_LIMIT
        ),
        cost_estimate=pl.CostEstimate(
            flops=0, bytes_accessed=50_000_000, transcendentals=0
        ),
        name=name,
    )(*args)


def stepped(kernel, name, steps, args, arg_specs, outs, out_specs, scratch, flops):
    return pl.pallas_call(
        kernel,
        grid=(steps,),
        out_shape=outs,
        in_specs=arg_specs,
        out_specs=out_specs,
        scratch_shapes=scratch,
        compiler_params=pltpu.CompilerParams(vmem_limit_bytes=VMEM_LIMIT),
        cost_estimate=pl.CostEstimate(
            flops=flops, bytes_accessed=20_000_000, transcendentals=0
        ),
        name=name,
    )(*args)


def shards(
    tokens, ln1_gain, ln1_shift, w_query, b_query, w_key, w_value, b_value, w_proj, b_proj,
    ln2_gain, ln2_shift, w_fc1, b_fc1, w_fc2, b_fc2, cotangent,
):
    images, length, width = tokens.shape
    assert images == lax.axis_size("tensor") == 4
    local = w_query.shape[1]
    hidden = w_fc1.shape[1]
    rows = (length + 15) // 16 * 16
    pad = ((0, 0), (0, rows - length), (0, 0))
    x = jnp.pad(tokens, pad)
    g = jnp.pad(cotangent, pad)
    full = (images, rows, width)
    thin = (images, rows, local)
    tall = (images, 2 * rows, width)
    count = lax.axis_size("dp")
    one, two = dp_orders(count)
    assert hidden == width and 4 * local == width and 1 << len(one) == count
    vec = jnp.stack([ln1_gain, ln1_shift, b_proj, ln2_gain, ln2_shift, b_fc2, b_fc1])
    bias = jnp.stack([b_query, b_value])

    normed, query, keys, values, mixed, part = stepped(
        lambda *refs: attention_kernel(length, *refs), "attention", images,
        (x, vec, bias, w_query, w_key, w_value, w_proj),
        [each(full), fixed(vec.shape), fixed(bias.shape)]
        + [fixed((width, local))] * 3 + [fixed((local, width))],
        [struct(full, BF16)] + [struct(thin, BF16)] * 4 + [struct(full, BF16)],
        [each(full)] + [each(thin)] * 4 + [each(full)],
        [], 2_000_000_000,
    )
    middle, resid = exchange(
        middle_kernel, 0, "middle", [struct(full, BF16), struct((rows, width), F32)], rows, width,
        [], (part, x, vec),
    )
    part, fc, grad_bfc1 = stepped(
        feed_kernel, "feed", images,
        (middle, g, w_fc1, vec, w_fc2),
        [each(full), each(full), fixed((width, hidden)), fixed(vec.shape),
         fixed((hidden, width))],
        [struct(tall, BF16), struct((width + hidden, width), BF16), struct((1, hidden), F32)],
        [each(tall), fixed((width + hidden, width)), fixed((1, hidden))],
        [pltpu.VMEM((width, hidden), F32), pltpu.VMEM((hidden, width), F32)], 6_000_000_000,
    )
    fc_land = landing_rows(width, one) + landing_rows(width, two)
    both, grad_resid, small, fc = exchange(
        lambda *refs: turn_kernel(count, *refs), 1, "turn",
        [struct(tall, BF16), struct((rows, width), F32), struct((8, width), F32),
         struct(fc.shape, BF16)],
        2 * rows, width, [pltpu.VMEM((fc_land, width), BF16)],
        (part, resid, g, vec, fc),
    )
    layer_out = both[:, :length]
    part, heads, grad_bias = stepped(
        lambda *refs: back_kernel(length, *refs), "back", images,
        (both, mixed, normed, query, keys, values, w_proj, w_query, w_key, w_value),
        [pl.BlockSpec((1, rows, width), lambda step: (step, 1, 0)), each(thin), each(full),
         each(thin), each(thin), each(thin), fixed((local, width))]
        + [fixed((width, local))] * 3,
        [struct(full, BF16), struct((width, width), BF16), struct((2, local), F32)],
        [each(full), fixed((width, width)), fixed((2, local))],
        [pltpu.VMEM((4, local, width), F32)], 4_000_000_000,
    )
    heads_land = landing_rows(width // 2, one) + landing_rows(width // 2, two)
    out, small, fc, heads = exchange(
        lambda *refs: last_kernel(count, *refs), 2, "last",
        [struct(full, BF16), struct((16, width), F32), struct(fc.shape, BF16),
         struct(heads.shape, BF16)],
        rows, width,
        [pltpu.VMEM(heads.shape, BF16), pltpu.VMEM((heads_land, width), BF16),
         pltpu.VMEM((3 + len(one), 16, width), F32),
         pltpu.VMEM((2 + len(one), 16, width), F32)],
        (part, x, grad_resid, vec, small, grad_bfc1, grad_bias, fc, heads),
    )
    tokens_grad = out[:, :length]
    heads = heads.astype(F32)
    fc = fc.astype(F32)
    square = lambda i: heads[i * local : (i + 1) * local]
    return (
        layer_out,
        tokens_grad,
        small[4],
        small[5],
        square(0).T,
        small[9, :local],
        square(1).T,
        square(2).T,
        small[10, :local],
        square(3),
        small[2],
        small[0],
        small[1],
        fc[:width],
        small[8, :hidden],
        fc[width:],
        small[3],
    )


def solution(mesh):
    in_specs = (
        P("dp", None, None),
        P(),
        P(),
        P(None, "tensor"),
        P("tensor"),
        P(None, "tensor"),
        P(None, "tensor"),
        P("tensor"),
        P("tensor", None),
        P(),
        P(),
        P(),
        P(None, "tensor"),
        P("tensor"),
        P("tensor", None),
        P(),
        P("dp", None, None),
    )
    out_specs = (
        P("dp", None, None),
        P("dp", None, None),
        P(),
        P(),
        P(None, "tensor"),
        P("tensor"),
        P(None, "tensor"),
        P(None, "tensor"),
        P("tensor"),
        P("tensor", None),
        P(),
        P(),
        P(),
        P(None, "tensor"),
        P("tensor"),
        P("tensor", None),
        P(),
    )
    return jax.shard_map(shards, mesh=mesh, in_specs=in_specs, out_specs=out_specs, check_vma=False)
```

time: 259 us -> 216 us (0.83)
  waiting for transfers between devices: 61.1 us -> 0 us
  Pallas kernels: 132 us -> 186 us
  starting transfers between devices: 18.1 us -> 0 us
  local copies, waits for them, and re-layouts: 37.1 us -> 27.3 us
  other arithmetic: 9.02 us -> 1.56 us
    ppermute x15 -> x0, waiting for transfers between devices: 61.1 us -> none  [the longest x6 29.1 us: sum_images(): got = lax.ppermute(current, 'dp', partners(count, distance))]
    pallas_call x3, Pallas kernels: 95.1 us -> 150 us  [exchange(): pl.pallas_call(kernel, out_shape=outs, in_specs=whole(len(args)), out_spe...]
    ppermute x15 -> x0, starting transfers between devices: 18.1 us -> none  [the longest x6 7.31 us: sum_images(): got = lax.ppermute(current, 'dp', partners(count, distance))]
    reshape x14 -> x0, local copies, waits for them, and re-layouts: 12.4 us -> none  [the longest x7 4.06 us: shards(): flat = lambda v: v.reshape(1, v.shape[0])]
    another operation x0 -> x8, local copies, waits for them, and re-layouts: none -> 5.46 us  [shards(): jnp.stack([ln1_gain, ln1_shift, b_proj, ln2_gain, ln2_shift, b_fc2, b_fc1])]
    add x7 -> x0, other arithmetic: 4.38 us -> none  [the longest x4 4.37 us: sum_images(): current = keep.astype(F32) + got.astype(F32)]
    unnamed x49 -> x17, local copies, waits for them, and re-layouts: 11.7 us -> 9.12 us
  transfers between devices with their start and end apart: 15 -> 0, of which waited for: 11 -> 0; matrix products, arithmetic and copies ran while one was open for 11% -> 0% of each run, Pallas kernels for 33% -> 0%
where the time goes in v2:
time: 216 us; the launch traced here: 215 us
  Pallas kernels  186 us (86%)
  local copies, waits for them, and re-layouts  27.3 us (13%)
    pallas_call x3, Pallas kernels, exchange(): pl.pallas_call(kernel, out_shape=outs, in_specs=whole(len(args)), out_spe...  150 us
    pallas_call x3, Pallas kernels, stepped(): pl.pallas_call(kernel, grid=(steps,), out_shape=outs, in_specs=arg_specs,...  35.8 us
    unnamed x17, local copies, waits for them, and re-layouts  9.12 us
    another operation x8, local copies, waits for them, and re-layouts, shards(): jnp.stack([ln1_gain, ln1_shift, b_proj, ln2_gain, ln2_shift, b_fc2, b_fc1])  5.46 us

profile of v2, /device:TPU:0, one launch (start us, length us, event | category | flops | bytes accessed | tf_op | source)
XLA Modules:
  0.0 215.2 jit_solution(273473840210628965)
XLA Ops:
  0.7 0.0 copy-start.4
  0.7 0.0 copy-start.2
  0.7 1.4 pad_maximum_fusion.refs_2_
  2.1 0.7 stack.33
  2.8 0.7 stack.34
  3.4 0.7 stack.35
  4.1 0.7 stack.36
  4.8 0.7 stack.37
  5.5 0.7 stack.39
  6.2 0.7 stack.38
  6.9 0.6 stack.40.refs_1_.vec.refs_3_
  7.5 1.9 copy.35.refs_3_.refs_7_
  9.4 1.9 copy.36.refs_4_.refs_8_
  11.3 0.0 copy-done.4
  11.3 0.9 copy.37.refs_5_.refs_9_
  12.2 0.0 copy-done.2
  12.2 0.1 copy.34
  12.3 0.0 copy-start.3
  12.3 1.1 pad.7.refs_0_.x_ref.refs_1_
  13.5 0.6 copy-done.3
  14.1 0.1 copy.38
  14.2 1.2 pad.8.g_ref.refs_2_
  15.4 9.1 %attention.1 = (bf16[4,208,768]{2,1,0:T(8,128)(2,1)}, bf16[4,208,192]{2,1,0:T(8,128)(2,1)}, bf16[4,208,192]{2,1,0:T(8,128)(2,1)}, bf16[4,208,192]{2,1,0:T(8,128)...) custom-call(bf16[4,208,768]{2,1,0:T(8,128)(2,1)} %pad.7.refs_0_.x_ref.refs_1_, ...), custom_call_target="tpu_custom_call" | custom-call | flops 2000000000 | bytes 20000000 | tf_op jit(solution)/shard_map/attention/pallas_call | solution.py:437
  24.5 27.4 %middle.1 = (bf16[4,208,768]{2,1,0:T(8,128)(2,1)}, f32[208,768]{1,0:T(8,128)}) custom-call(bf16[4,208,768]{2,1,0:T(8,128)(2,1)} %get-tuple-element.39.part, bf16[4,208,768]{2,1,0:T(8,128)(2,1)} %pad.7.refs_0_.x_ref.refs_1_, f32[7,768]{1,0:T(8,128)} %stack.40.refs_1_.vec.refs_3_), custom_call_target="tpu_custom_call" | custom-call | bytes 50000000 | tf_op jit(solution)/shard_map/middle/pallas_call | solution.py:414
  51.9 12.2 %feed.1 = (bf16[4,416,768]{2,1,0:T(8,128)(2,1)}, bf16[1536,768]{1,0:T(8,128)(2,1)}, f32[1,768]{1,0:T(1,128)}) custom-call(bf16[4,208,768]{2,1,0:T(8,128)(2,1)} %get-tuple-element.40.c_ref, bf16[4,208,768]{2,1,0:T(8,128)(2,1)} %pad.8.g_ref.refs_2_, bf16[768,768]{1,0:T(8,128)(2,1)} %w1.1, f32[7,768]{1,0:T(8,128)} %stack.40.refs_1_.vec.refs_3_, bf16[768,768]{1,0:T(8,128)(2,1)} %w2.1), custom_call_target="tpu_custom_call" | custom-call | flops 6000000000 | bytes 20000000 | tf_op jit(solution)/shard_map/feed/pallas_call | solution.py:437
  64.1 45.8 %turn.1 = (bf16[4,416,768]{2,1,0:T(8,128)(2,1)}, f32[208,768]{1,0:T(8,128)}, f32[8,768]{1,0:T(8,128)}, bf16[1536,768]{1,0:T(8,128)(2,1)}) custom-call(bf16[4,416,768]{2,1,0:T(8,128)(2,1)} %get-tuple-element.41.refs_0_, f32[208,768]{1,0:T(8,128)} %get-tuple-element.42.refs_1_, bf16[4,208,768]{2,1,0:T(8,128)(2,1)} %pad.8.g_ref.refs_2_, ...), custom_call_target="tpu_custom_call" | custom-call | bytes 50000000 | tf_op jit(solution)/shard_map/turn/pallas_call | solution.py:414
  110.0 14.6 %back.1 = (bf16[4,208,768]{2,1,0:T(8,128)(2,1)}, bf16[768,768]{1,0:T(8,128)(2,1)}, f32[2,192]{1,0:T(2,128)}) custom-call(bf16[4,416,768]{2,1,0:T(8,128)(2,1)} %get-tuple-element.44.refs_0_, bf16[4,208,192]{2,1,0:T(8,128)(2,1)} %get-tuple-element.45.refs_1_, bf16[4,208,768]{2,1,0:T(8,128)(2,1)} %get-tuple-element.46.refs_2_, ...), custom_call_target="tpu_custom_call" | custom-call | flops 4000000000 | bytes 20000000 | tf_op jit(solution)/shard_map/back/pallas_call | solution.py:437
  124.5 76.5 %last.1 = (bf16[4,208,768]{2,1,0:T(8,128)(2,1)}, f32[16,768]{1,0:T(8,128)}, bf16[1536,768]{1,0:T(8,128)(2,1)}, bf16[768,768]{1,0:T(8,128)(2,1)}) custom-call(bf16[4,208,768]{2,1,0:T(8,128)(2,1)} %get-tuple-element.50.refs_0_, bf16[4,208,768]{2,1,0:T(8,128)(2,1)} %pad.7.refs_0_.x_ref.refs_1_, f32[208,768]{1,0:T(8,128)} %get-tuple-element.51.refs_2_, ...), custom_call_target="tpu_custom_call" | custom-call | bytes 50000000 | tf_op jit(solution)/shard_map/last/pallas_call | solution.py:414
  201.0 1.4 slice.52
  202.4 0.0 copy-start.1
  202.4 1.5 copy.43
  203.9 1.3 fusion.1
  205.2 1.6 slice_reduce_fusion
  206.9 0.0 copy-done.1
  206.9 0.9 slice.71
  207.7 0.2 convert_element_type.9
  207.9 1.2 slice_bitcast_fusion
  209.1 1.4 slice.51
  210.5 0.0 copy-start
  210.5 1.5 copy.42
  212.0 0.6 copy-done
  212.6 2.5 %fusion = (f32[768,768]{1,0:T(8,128)}, f32[768,768]{1,0:T(8,128)}) fusion(bf16[1536,768]{1,0:T(8,128)(2,1)S(1)} %copy-done), kind=kLoop, calls=%fused_computation.11 | loop fusion | bytes 9437184 | tf_op jit(solution)/shard_map/slice | solution.py:545
Async XLA Ops:
  0.7 10.6 %copy-start.4 = (bf16[768,192]{0,1:T(8,128)(2,1)S(1)}, bf16[768,192]{0,1:T(8,128)(2,1)}, u32[]{:S(2)}) copy-start(bf16[768,192]{0,1:T(8,128)(2,1)} %param.23) | copy-start | bytes 884740
  0.7 11.5 %copy-start.2 = (bf16[4,197,768]{2,0,1:T(4,128)(2,1)S(1)}, bf16[4,197,768]{2,0,1:T(4,128)(2,1)}, u32[]{:S(2)}) copy-start(bf16[4,197,768]{2,0,1:T(4,128)(2,1)} %param.17) | copy-start | bytes 3631108
  12.3 1.7 copy-start.3
  202.4 4.5 %copy-start.1 = (bf16[768,768]{1,0:T(8,128)(2,1)S(1)}, bf16[768,768]{1,0:T(8,128)(2,1)}, u32[]{:S(2)}) copy-start(bf16[768,768]{1,0:T(8,128)(2,1)} %get-tuple-element.59) | copy-start | bytes 3538948
  210.5 2.1 copy-start

commit v3 on v2

--- a/solution.py
+++ b/solution.py
@@ -40,6 +40,10 @@
     )
 
 
+def line(ref):
+    return ref[...].reshape(1, ref.shape[0])
+
+
 def soft_probs(query, keys, length):
     scores = times_transpose(query, keys) * (HEAD_DIM**-0.5)
     column = lax.broadcasted_iota(jnp.int32, scores.shape, 1)
@@ -49,14 +53,14 @@
 
 
 def attention_kernel(
-    length, x_ref, vec, bias, wq, wk, wv, wp, a_ref, q_ref, k_ref, v_ref, o_ref, part_ref
+    length, x_ref, gain, shift, bq, bv, wq, wk, wv, wp, a_ref, q_ref, k_ref, v_ref, o_ref, part_ref
 ):
     hat, _ = normalize(x_ref[0].astype(F32))
-    normed = (hat * vec[0:1] + vec[1:2]).astype(BF16)
+    normed = (hat * line(gain) + line(shift)).astype(BF16)
     a_ref[0] = normed
-    query = (matmul(normed, wq[...]) + bias[0:1]).astype(BF16)
-    keys = matmul(normed, wk[...]).astype(BF16)
-    values = (matmul(normed, wv[...]) + bias[1:2]).astype(BF16)
+    query = (times_transpose(normed, wq[...]) + line(bq)).astype(BF16)
+    keys = times_transpose(normed, wk[...]).astype(BF16)
+    values = (times_transpose(normed, wv[...]) + line(bv)).astype(BF16)
     q_ref[0] = query
     k_ref[0] = keys
     v_ref[0] = values
@@ -70,7 +74,7 @@
     part_ref[0] = matmul(mixed, wp[...]).astype(BF16)
 
 
-def feed_kernel(c_ref, g_ref, w1, vec, w2, part_ref, fc_ref, bias_ref, acc1, acc2):
+def feed_kernel(c_ref, g_ref, w1, b1, w2, part_ref, fc_ref, bias_ref, acc1, acc2):
     step = pl.program_id(0)
     rows = c_ref.shape[1]
     width = c_ref.shape[2]
@@ -83,7 +87,7 @@
 
     middle = c_ref[0]
     grad = g_ref[0]
-    hidden = matmul(middle, w1[...]) + vec[6:7]
+    hidden = matmul(middle, w1[...]) + line(b1)
     cdf = 0.5 * (1.0 + lax.erf(hidden * (0.5**0.5)))
     slope = cdf + hidden * jnp.exp(-0.5 * hidden * hidden) * 0.3989422804014327
     active = (hidden * cdf).astype(BF16)
@@ -100,22 +104,19 @@
         fc_ref[width:] = acc2[...].astype(BF16)
 
 
-def back_kernel(
-    length, h_ref, o_ref, a_ref, q_ref, k_ref, v_ref, wp, wq, wk, wv,
-    part_ref, grads_ref, bias_ref, acc,
+def image_back(
+    length, image, start, h_ref, o_ref, a_ref, q_ref, k_ref, v_ref, wp, wq, wk, wv,
+    part_ref, bias_ref, acc,
 ):
-    step = pl.program_id(0)
-
-    @pl.when(step == 0)
-    def _():
-        acc[...] = jnp.zeros_like(acc)
-        bias_ref[...] = jnp.zeros_like(bias_ref)
-
-    low = h_ref[0]
-    acc[3] += inner_rows(o_ref[0], low)
+    def add(ref, index, value):
+        ref[index] = value if start else ref[index] + value
+
+    rows = a_ref.shape[1]
+    low = h_ref[image, rows:]
+    add(acc, 3, inner_rows(o_ref[image], low))
     grad_mixed = times_transpose(low, wp[...]).astype(BF16)
-    normed = a_ref[0]
-    query, keys, values = q_ref[0], k_ref[0], v_ref[0]
+    normed = a_ref[image]
+    query, keys, values = q_ref[image], k_ref[image], v_ref[image]
     score_scale = HEAD_DIM**-0.5
     dq, dk, dv = [], [], []
     for head in range(query.shape[1] // HEAD_DIM):
@@ -131,20 +132,14 @@
     dq = jnp.concatenate(dq, axis=1).astype(BF16)
     dk = jnp.concatenate(dk, axis=1).astype(BF16)
     dv = jnp.concatenate(dv, axis=1).astype(BF16)
-    bias_ref[0:1] += jnp.sum(dq.astype(F32), axis=0, keepdims=True)
-    bias_ref[1:2] += jnp.sum(dv.astype(F32), axis=0, keepdims=True)
-    part_ref[0] = (
-        times_transpose(dq, wq[...]) + times_transpose(dk, wk[...]) + times_transpose(dv, wv[...])
+    add(bias_ref, slice(0, 1), jnp.sum(dq.astype(F32), axis=0, keepdims=True))
+    add(bias_ref, slice(1, 2), jnp.sum(dv.astype(F32), axis=0, keepdims=True))
+    part_ref[image] = (
+        matmul(dq, wq[...]) + matmul(dk, wk[...]) + matmul(dv, wv[...])
     ).astype(BF16)
-    acc[0] += inner_rows(dq, normed)
-    acc[1] += inner_rows(dk, normed)
-    acc[2] += inner_rows(dv, normed)
-
-    @pl.when(step == pl.num_programs(0) - 1)
-    def _():
-        local = acc.shape[1]
-        for index in range(4):
-            grads_ref[index * local : (index + 1) * local] = acc[index].astype(BF16)
+    add(acc, 0, inner_rows(dq, normed))
+    add(acc, 1, inner_rows(dk, normed))
+    add(acc, 2, inner_rows(dv, normed))
 
 
 def places():
@@ -241,18 +236,19 @@
     yield from spread_up(send, result, steps)
 
 
-def landing_rows(size, distances):
-    return sum(rows for _, _, _, rows, _ in halvings(0, size, distances))
-
-
-def reduce_share(send, part, near_in, out_buf, far_in):
+def reduce_share(send, part, near_in, out_buf, far_in, prepare=None):
     here, near, far, diag = places()
+    ready = prepare or (lambda image, start: None)
+    ready(diag, True)
     first = send(part.at[diag], near_in.at[0], {"tensor": near})
+    ready(near, False)
     second = send(part.at[near], near_in.at[1], {"tensor": near})
     yield
+    ready(far, False)
     first.wait_recv()
     out_buf[...] = (part[far].astype(F32) + near_in[0].astype(F32)).astype(BF16)
     third = send(out_buf, far_in, {"tensor": far})
+    ready(here, False)
     yield
     second.wait_recv()
     near_sum = part[here].astype(F32) + near_in[1].astype(F32)
@@ -284,37 +280,47 @@
     return [{"tensor": near}, {"tensor": far}]
 
 
-def dp_orders(count):
-    distances = [1 << i for i in range(count.bit_length() - 1)]
-    return distances, distances[1:] + distances[:1]
-
-
-def middle_kernel(part, x_ref, vec, out, h_ref, near_in, out_buf, far_in, sems):
+def dp_distances(count):
+    return [1 << i for i in range(count.bit_length() - 1)]
+
+
+def streams(rows, count, parts):
+    one = dp_distances(count)
+    orders = [one, one[1:] + one[:1]]
+    size = rows // parts
+    found, at = [], 0
+    for index in range(parts):
+        steps = halvings(index * size, size, orders[index % 2])
+        found.append((at, steps))
+        at += sum(step[3] for step in steps)
+    return found, at
+
+
+def middle_kernel(part, x_ref, bias, gain, shift, out, h_ref, near_in, out_buf, far_in, sems):
     here, near, far, _ = places()
     send = Sender(sems)
     greet(tensor_others())
 
     def task():
         total = yield from reduce_share(send, part, near_in, out_buf, far_in)
-        resid = x_ref[here].astype(F32) + total + vec[2:3]
+        resid = x_ref[here].astype(F32) + total + line(bias)
         h_ref[...] = resid
         hat, _ = normalize(resid)
-        out[here] = (hat * vec[3:4] + vec[4:5]).astype(BF16)
+        out[here] = (hat * line(gain) + line(shift)).astype(BF16)
         yield from gather_share(send, out)
 
     take_turns([task()])
 
 
 def turn_kernel(
-    count, part, h_ref, g_ref, vec, fc, out, dh_ref, small, work,
+    count, part, h_ref, g_ref, bias, gain, fc, out, dh_ref, small, work,
     near_in, out_buf, far_in, sems, landing,
 ):
     here = lax.axis_index("tensor")
     rows = h_ref.shape[0]
     send = Sender(sems)
-    one, two = dp_orders(count)
-    greet(tensor_others() + [{"dp": mirror(d)} for d in one])
-    half = fc.shape[0] // 2
+    greet(tensor_others() + [{"dp": mirror(d)} for d in dp_distances(count)])
+    found, _ = streams(fc.shape[0], count, 4)
 
     def task():
         total = yield from reduce_share(send, part, near_in, out_buf, far_in)
@@ -322,9 +328,9 @@
         grad = total[rows:]
         own = g_ref[here].astype(F32)
         hat, scale = normalize(resid)
-        grad_resid = own + norm_back(hat, scale, vec[3:4], grad)
+        grad_resid = own + norm_back(hat, scale, line(gain), grad)
         dh_ref[...] = grad_resid
-        out[here, :rows] = (resid + total[:rows] + vec[5:6]).astype(BF16)
+        out[here, :rows] = (resid + total[:rows] + line(bias)).astype(BF16)
         out[here, rows:] = grad_resid.astype(BF16)
         small[0:1] = jnp.sum(grad * hat, axis=0, keepdims=True)
         small[1:2] = jnp.sum(grad, axis=0, keepdims=True)
@@ -335,32 +341,38 @@
 
     take_turns([
         task(),
-        sum_down(send, fc, work, landing, 0, halvings(0, half, one)),
-        sum_down(send, fc, work, landing, landing_rows(half, one), halvings(half, half, two)),
+        *(sum_down(send, fc, work, landing, at, steps) for at, steps in found),
     ])
 
 
 def last_kernel(
-    count, part, x_ref, dh_ref, vec, small_in, bfc1, bqv, fc, heads,
+    count, length, both, mixed, normed, query, keys, values, wp, wq, wk, wv,
+    x_ref, dh_ref, gain, small_in, bfc1, fc,
     out, small, fc_out, heads_out,
-    near_in, out_buf, far_in, sems, work, landing, sums, got,
+    near_in, out_buf, far_in, sems, part, acc, bias, heads, work, landing, sums, got,
 ):
     here, near, far, _ = places()
     send = Sender(sems)
-    one, two = dp_orders(count)
-    greet(tensor_others() + [{"dp": mirror(d)} for d in one])
-    fc_half = fc.shape[0] // 2
-    half = heads.shape[0] // 2
-    local = bqv.shape[1]
-    fc_steps = halvings(0, fc_half, one), halvings(fc_half, fc_half, two)
-    for steps in fc_steps:
+    distances = dp_distances(count)
+    greet(tensor_others() + [{"dp": mirror(d)} for d in distances])
+    local = wp.shape[0]
+    fc_streams, _ = streams(fc.shape[0], count, 4)
+    head_streams, _ = streams(heads.shape[0], count, 2)
+    for _, steps in fc_streams:
         _, kept, _, rows, _ = steps[-1]
         fc_out[span(kept, rows)] = fc[span(kept, rows)]
+    sums[0, 8:16] = jnp.zeros((8, sums.shape[2]), F32)
+
+    def prepare(image, start):
+        image_back(
+            length, image, start, both, mixed, normed, query, keys, values,
+            wp, wq, wk, wv, part, bias, acc,
+        )
 
     def task():
-        total = yield from reduce_share(send, part, near_in, out_buf, far_in)
+        total = yield from reduce_share(send, part, near_in, out_buf, far_in, prepare)
         hat, scale = normalize(x_ref[here].astype(F32))
-        out[here] = (dh_ref[...] + norm_back(hat, scale, vec[0:1], total)).astype(BF16)
+        out[here] = (dh_ref[...] + norm_back(hat, scale, line(gain), total)).astype(BF16)
         sums[0, :8] = small_in[...]
         sums[0, 4:5] = jnp.sum(total * hat, axis=0, keepdims=True)
         sums[0, 5:6] = jnp.sum(total, axis=0, keepdims=True)
@@ -373,24 +385,25 @@
         copy.wait()
         sums[2] = sums[1] + got[1]
         sums[2, 8:9] = bfc1[...]
-        sums[2, 9:11, :local] = bqv[...]
-        for slot, distance in enumerate(one, 2):
+        sums[2, 9:11, :local] = bias[...]
+        for slot, distance in enumerate(distances, 2):
             copy = send(sums.at[slot], got.at[slot], {"dp": mirror(distance)})
             yield
             copy.wait()
             sums[slot + 1] = sums[slot] + got[slot]
-        small[...] = sums[len(one) + 2]
-
-    sums[0, 8:16] = jnp.zeros((8, sums.shape[2]), F32)
+        small[...] = sums[len(distances) + 2]
+
+    def head_task(index, at, steps):
+        yield
+        if index == 0:
+            for block in range(4):
+                heads[block * local : (block + 1) * local] = acc[block].astype(BF16)
+        yield from sum_all(send, heads, work, heads_out, landing, at, steps)
+
     take_turns([
+        *(spread_up(send, fc_out, steps) for _, steps in fc_streams),
         task(),
-        spread_up(send, fc_out, fc_steps[0]),
-        spread_up(send, fc_out, fc_steps[1]),
-        sum_all(send, heads, work, heads_out, landing, 0, halvings(0, half, one)),
-        sum_all(
-            send, heads, work, heads_out, landing, landing_rows(half, one),
-            halvings(half, half, two),
-        ),
+        *(head_task(i, at, steps) for i, (at, steps) in enumerate(head_streams)),
     ])
 
 
@@ -465,62 +478,54 @@
     thin = (images, rows, local)
     tall = (images, 2 * rows, width)
     count = lax.axis_size("dp")
-    one, two = dp_orders(count)
-    assert hidden == width and 4 * local == width and 1 << len(one) == count
-    vec = jnp.stack([ln1_gain, ln1_shift, b_proj, ln2_gain, ln2_shift, b_fc2, b_fc1])
-    bias = jnp.stack([b_query, b_value])
+    distances = dp_distances(count)
+    assert hidden == width and 4 * local == width and 1 << len(distances) == count
+    turned = [weight.T for weight in (w_query, w_key, w_value)]
 
     normed, query, keys, values, mixed, part = stepped(
         lambda *refs: attention_kernel(length, *refs), "attention", images,
-        (x, vec, bias, w_query, w_key, w_value, w_proj),
-        [each(full), fixed(vec.shape), fixed(bias.shape)]
-        + [fixed((width, local))] * 3 + [fixed((local, width))],
+        (x, ln1_gain, ln1_shift, b_query, b_value, *turned, w_proj),
+        [each(full)] + [fixed((width,))] * 2 + [fixed((local,))] * 2
+        + [fixed((local, width))] * 4,
         [struct(full, BF16)] + [struct(thin, BF16)] * 4 + [struct(full, BF16)],
         [each(full)] + [each(thin)] * 4 + [each(full)],
         [], 2_000_000_000,
     )
     middle, resid = exchange(
         middle_kernel, 0, "middle", [struct(full, BF16), struct((rows, width), F32)], rows, width,
-        [], (part, x, vec),
+        [], (part, x, b_proj, ln2_gain, ln2_shift),
     )
     part, fc, grad_bfc1 = stepped(
         feed_kernel, "feed", images,
-        (middle, g, w_fc1, vec, w_fc2),
-        [each(full), each(full), fixed((width, hidden)), fixed(vec.shape),
+        (middle, g, w_fc1, b_fc1, w_fc2),
+        [each(full), each(full), fixed((width, hidden)), fixed((hidden,)),
          fixed((hidden, width))],
         [struct(tall, BF16), struct((width + hidden, width), BF16), struct((1, hidden), F32)],
         [each(tall), fixed((width + hidden, width)), fixed((1, hidden))],
         [pltpu.VMEM((width, hidden), F32), pltpu.VMEM((hidden, width), F32)], 6_000_000_000,
     )
-    fc_land = landing_rows(width, one) + landing_rows(width, two)
+    _, land = streams(width + hidden, count, 4)
     both, grad_resid, small, fc = exchange(
         lambda *refs: turn_kernel(count, *refs), 1, "turn",
         [struct(tall, BF16), struct((rows, width), F32), struct((8, width), F32),
          struct(fc.shape, BF16)],
-        2 * rows, width, [pltpu.VMEM((fc_land, width), BF16)],
-        (part, resid, g, vec, fc),
+        2 * rows, width, [pltpu.VMEM((land, width), BF16)],
+        (part, resid, g, b_fc2, ln2_gain, fc),
     )
     layer_out = both[:, :length]
-    part, heads, grad_bias = stepped(
-        lambda *refs: back_kernel(length, *refs), "back", images,
-        (both, mixed, normed, query, keys, values, w_proj, w_query, w_key, w_value),
-        [pl.BlockSpec((1, rows, width), lambda step: (step, 1, 0)), each(thin), each(full),
-         each(thin), each(thin), each(thin), fixed((local, width))]
-        + [fixed((width, local))] * 3,
-        [struct(full, BF16), struct((width, width), BF16), struct((2, local), F32)],
-        [each(full), fixed((width, width)), fixed((2, local))],
-        [pltpu.VMEM((4, local, width), F32)], 4_000_000_000,
-    )
-    heads_land = landing_rows(width // 2, one) + landing_rows(width // 2, two)
+    _, land = streams(width, count, 2)
     out, small, fc, heads = exchange(
-        lambda *refs: last_kernel(count, *refs), 2, "last",
+        lambda *refs: last_kernel(count, length, *refs), 2, "last",
         [struct(full, BF16), struct((16, width), F32), struct(fc.shape, BF16),
-         struct(heads.shape, BF16)],
+         struct((width, width), BF16)],
         rows, width,
-        [pltpu.VMEM(heads.shape, BF16), pltpu.VMEM((heads_land, width), BF16),
-         pltpu.VMEM((3 + len(one), 16, width), F32),
-         pltpu.VMEM((2 + len(one), 16, width), F32)],
-        (part, x, grad_resid, vec, small, grad_bfc1, grad_bias, fc, heads),
+        [pltpu.VMEM(full, BF16), pltpu.VMEM((4, local, width), F32),
+         pltpu.VMEM((2, local), F32), pltpu.VMEM((width, width), BF16),
+         pltpu.VMEM((width, width), BF16), pltpu.VMEM((land, width), BF16),
+         pltpu.VMEM((3 + len(distances), 16, width), F32),
+         pltpu.VMEM((2 + len(distances), 16, width), F32)],
+        (both, mixed, normed, query, keys, values, w_proj, *turned,
+         x, grad_resid, ln1_gain, small, grad_bfc1, fc),
     )
     tokens_grad = out[:, :length]
     heads = heads.astype(F32)

time: 216 us -> 194 us (0.90)
  Pallas kernels: 186 us -> 175 us
  local copies, waits for them, and re-layouts: 27.3 us -> 17.6 us
    pallas_call x3 -> x2, Pallas kernels: 35.8 us -> 21.2 us  [stepped(): pl.pallas_call(kernel, grid=(steps,), out_shape=outs, in_specs=arg_specs,...]
    another operation x8 -> x0, local copies, waits for them, and re-layouts: 5.46 us -> none  [shards(): jnp.stack([ln1_gain, ln1_shift, b_proj, ln2_gain, ln2_shift, b_fc2, b_fc1])]
    pallas_call x3, Pallas kernels: 150 us -> 153 us  [exchange(): pl.pallas_call(kernel, out_shape=outs, in_specs=whole(len(args)), out_spe...]
    unnamed x17 -> x12, local copies, waits for them, and re-layouts: 9.12 us -> 6.18 us
where the time goes in v3:
time: 194 us; the launch traced here: 193 us
  Pallas kernels  175 us (90%)
  local copies, waits for them, and re-layouts  17.6 us (9%)
    pallas_call x3, Pallas kernels, exchange(): pl.pallas_call(kernel, out_shape=outs, in_specs=whole(len(args)), out_spe...  153 us
    pallas_call x2, Pallas kernels, stepped(): pl.pallas_call(kernel, grid=(steps,), out_shape=outs, in_specs=arg_specs,...  21.2 us
    unnamed x12, local copies, waits for them, and re-layouts  6.18 us

profile of v3, /device:TPU:0, one launch (start us, length us, event | category | flops | bytes accessed | tf_op | source)
XLA Modules:
  0.0 193.2 jit_solution(481813702490918905)
XLA Ops:
  0.7 1.4 copy.34
  2.1 0.0 copy-start.2
  2.1 1.1 pad.7.refs_0_.x_ref.refs_10_
  3.2 0.6 copy-done.2
  3.8 0.1 copy.35
  3.9 1.1 pad.8.g_ref.refs_2_
  5.1 9.1 %attention.1 = (bf16[4,208,768]{2,1,0:T(8,128)(2,1)}, bf16[4,208,192]{2,1,0:T(8,128)(2,1)}, bf16[4,208,192]{2,1,0:T(8,128)(2,1)}, bf16[4,208,192]{2,1,0:T(8,128)...) custom-call(bf16[4,208,768]{2,1,0:T(8,128)(2,1)} %pad.7.refs_0_.x_ref.refs_10_, f32[768]{0:T(1024)} %refs_12_.1, ...), custom_call_target="tpu_custom_call" | custom-call | flops 2000000000 | bytes 20000000 | tf_op jit(solution)/shard_map/attention/pallas_call | solution.py:450
  14.1 27.4 %middle.1 = (bf16[4,208,768]{2,1,0:T(8,128)(2,1)}, f32[208,768]{1,0:T(8,128)}) custom-call(bf16[4,208,768]{2,1,0:T(8,128)(2,1)} %get-tuple-element.36.part, bf16[4,208,768]{2,1,0:T(8,128)(2,1)} %pad.7.refs_0_.x_ref.refs_10_, f32[768]{0:T(1024)} %bias.1, f32[768]{0:T(1024)} %refs_4_.3, f32[768]{0:T(1024)} %shift.1), custom_call_target="tpu_custom_call" | custom-call | bytes 50000000 | tf_op jit(solution)/shard_map/middle/pallas_call | solution.py:427
  41.5 12.2 %feed.1 = (bf16[4,416,768]{2,1,0:T(8,128)(2,1)}, bf16[1536,768]{1,0:T(8,128)(2,1)}, f32[1,768]{1,0:T(1,128)}) custom-call(bf16[4,208,768]{2,1,0:T(8,128)(2,1)} %get-tuple-element.37.c_ref, bf16[4,208,768]{2,1,0:T(8,128)(2,1)} %pad.8.g_ref.refs_2_, bf16[768,768]{1,0:T(8,128)(2,1)} %w1.1, f32[768]{0:T(1024)} %b1.1, bf16[768,768]{1,0:T(8,128)(2,1)} %w2.1), custom_call_target="tpu_custom_call" | custom-call | flops 6000000000 | bytes 20000000 | tf_op jit(solution)/shard_map/feed/pallas_call | solution.py:450
  53.7 45.3 %turn.1 = (bf16[4,416,768]{2,1,0:T(8,128)(2,1)}, f32[208,768]{1,0:T(8,128)}, f32[8,768]{1,0:T(8,128)}, bf16[1536,768]{1,0:T(8,128)(2,1)}) custom-call(bf16[4,416,768]{2,1,0:T(8,128)(2,1)} %get-tuple-element.38.refs_0_, f32[208,768]{1,0:T(8,128)} %get-tuple-element.39.refs_1_, bf16[4,208,768]{2,1,0:T(8,128)(2,1)} %pad.8.g_ref.refs_2_, f32[768]{0:T(1024)} %refs_3_.3, ...), custom_call_target="tpu_custom_call" | custom-call | bytes 50000000 | tf_op jit(solution)/shard_map/turn/pallas_call | solution.py:427
  99.0 80.7 %last.1 = (bf16[4,208,768]{2,1,0:T(8,128)(2,1)}, f32[16,768]{1,0:T(8,128)}, bf16[1536,768]{1,0:T(8,128)(2,1)}, bf16[768,768]{1,0:T(8,128)(2,1)}) custom-call(bf16[4,416,768]{2,1,0:T(8,128)(2,1)} %get-tuple-element.41.refs_0_, bf16[4,208,192]{2,1,0:T(8,128)(2,1)} %get-tuple-element.42.refs_1_, bf16[4,208,768]{2,1,0:T(8,128)(2,1)} %get-tuple-element.43.refs_2_, ...), custom_call_target="tpu_custom_call" | custom-call | bytes 50000000 | tf_op jit(solution)/shard_map/last/pallas_call | solution.py:427
  179.8 1.4 slice.51
  181.1 0.0 copy-start.3
  181.1 1.5 copy.36
  182.6 0.0 copy-done.3
  182.6 0.1 slice.52
  182.7 0.0 copy-start.1
  182.7 1.5 copy.37
  184.2 1.3 fusion.1
  185.6 1.7 slice_reduce_fusion
  187.3 0.0 copy-done.1
  187.3 0.9 slice.71
  188.1 0.2 convert_element_type.9
  188.3 0.0 copy-start
  188.3 1.2 slice_bitcast_fusion
  189.6 1.1 copy-done
  190.6 2.5 %fusion = (f32[768,768]{1,0:T(8,128)}, f32[768,768]{1,0:T(8,128)}) fusion(bf16[1536,768]{1,0:T(8,128)(2,1)S(1)} %copy-done), kind=kLoop, calls=%fused_computation.10 | loop fusion | bytes 9437184 | tf_op jit(solution)/shard_map/slice | solution.py:550
Async XLA Ops:
  2.1 1.7 copy-start.2
  181.1 1.5 copy-start.3
  182.7 4.6 %copy-start.1 = (bf16[768,768]{1,0:T(8,128)(2,1)S(1)}, bf16[768,768]{1,0:T(8,128)(2,1)}, u32[]{:S(2)}) copy-start(bf16[768,768]{1,0:T(8,128)(2,1)} %get-tuple-element.53) | copy-start | bytes 3538948
  188.3 2.3 %copy-start = (bf16[1536,768]{1,0:T(8,128)(2,1)S(1)}, bf16[1536,768]{1,0:T(8,128)(2,1)}, u32[]{:S(2)}) copy-start(bf16[1536,768]{1,0:T(8,128)(2,1)} %get-tuple-element.54) | copy-start | bytes 7077892

commit v4 on v3

--- a/solution.py
+++ b/solution.py
@@ -74,9 +74,8 @@
     part_ref[0] = matmul(mixed, wp[...]).astype(BF16)
 
 
-def feed_kernel(c_ref, g_ref, w1, b1, w2, part_ref, fc_ref, bias_ref, acc1, acc2):
+def feed_kernel(c_ref, g_ref, w1, b1, w2, part_ref, branch_ref, fc_ref, bias_ref, acc1, acc2):
     step = pl.program_id(0)
-    rows = c_ref.shape[1]
     width = c_ref.shape[2]
 
     @pl.when(step == 0)
@@ -92,8 +91,8 @@
     slope = cdf + hidden * jnp.exp(-0.5 * hidden * hidden) * 0.3989422804014327
     active = (hidden * cdf).astype(BF16)
     grad_hidden = (times_transpose(grad, w2[...]) * slope).astype(BF16)
-    part_ref[0, :rows] = matmul(active, w2[...]).astype(BF16)
-    part_ref[0, rows:] = times_transpose(grad_hidden, w1[...]).astype(BF16)
+    branch_ref[0] = matmul(active, w2[...]).astype(BF16)
+    part_ref[0] = times_transpose(grad_hidden, w1[...]).astype(BF16)
     acc2[...] += inner_rows(active, grad)
     acc1[...] += inner_rows(middle, grad_hidden)
     bias_ref[...] += jnp.sum(grad_hidden.astype(F32), axis=0, keepdims=True)
@@ -111,8 +110,7 @@
     def add(ref, index, value):
         ref[index] = value if start else ref[index] + value
 
-    rows = a_ref.shape[1]
-    low = h_ref[image, rows:]
+    low = h_ref[image]
     add(acc, 3, inner_rows(o_ref[image], low))
     grad_mixed = times_transpose(low, wp[...]).astype(BF16)
     normed = a_ref[image]
@@ -313,25 +311,21 @@
 
 
 def turn_kernel(
-    count, part, h_ref, g_ref, bias, gain, fc, out, dh_ref, small, work,
+    count, part, h_ref, g_ref, gain, fc, out, dh_ref, small, work,
     near_in, out_buf, far_in, sems, landing,
 ):
     here = lax.axis_index("tensor")
-    rows = h_ref.shape[0]
     send = Sender(sems)
     greet(tensor_others() + [{"dp": mirror(d)} for d in dp_distances(count)])
     found, _ = streams(fc.shape[0], count, 4)
 
     def task():
-        total = yield from reduce_share(send, part, near_in, out_buf, far_in)
-        resid = h_ref[...]
-        grad = total[rows:]
+        grad = yield from reduce_share(send, part, near_in, out_buf, far_in)
         own = g_ref[here].astype(F32)
-        hat, scale = normalize(resid)
+        hat, scale = normalize(h_ref[...])
         grad_resid = own + norm_back(hat, scale, line(gain), grad)
         dh_ref[...] = grad_resid
-        out[here, :rows] = (resid + total[:rows] + line(bias)).astype(BF16)
-        out[here, rows:] = grad_resid.astype(BF16)
+        out[here] = grad_resid.astype(BF16)
         small[0:1] = jnp.sum(grad * hat, axis=0, keepdims=True)
         small[1:2] = jnp.sum(grad, axis=0, keepdims=True)
         small[2:3] = jnp.sum(grad_resid, axis=0, keepdims=True)
@@ -346,10 +340,10 @@
 
 
 def last_kernel(
-    count, length, both, mixed, normed, query, keys, values, wp, wq, wk, wv,
-    x_ref, dh_ref, gain, small_in, bfc1, fc,
-    out, small, fc_out, heads_out,
-    near_in, out_buf, far_in, sems, part, acc, bias, heads, work, landing, sums, got,
+    count, length, grads_in, mixed, normed, query, keys, values, wp, wq, wk, wv,
+    x_ref, dh_ref, gain, small_in, bfc1, fc, branch, h_ref, bias_out,
+    out, small, fc_out, heads_out, layer,
+    near_in, out_buf, far_in, sems, near_two, out_two, far_two, part, acc, bias, heads, work, landing, sums, got,
 ):
     here, near, far, _ = places()
     send = Sender(sems)
@@ -365,7 +359,7 @@
 
     def prepare(image, start):
         image_back(
-            length, image, start, both, mixed, normed, query, keys, values,
+            length, image, start, grads_in, mixed, normed, query, keys, values,
             wp, wq, wk, wv, part, bias, acc,
         )
 
@@ -393,6 +387,11 @@
             sums[slot + 1] = sums[slot] + got[slot]
         small[...] = sums[len(distances) + 2]
 
+    def layer_task():
+        total = yield from reduce_share(send, branch, near_two, out_two, far_two)
+        layer[here] = (h_ref[...] + total + line(bias_out)).astype(BF16)
+        yield from gather_share(send, layer)
+
     def head_task(index, at, steps):
         yield
         if index == 0:
@@ -402,6 +401,7 @@
 
     take_turns([
         *(spread_up(send, fc_out, steps) for _, steps in fc_streams),
+        layer_task(),
         task(),
         *(head_task(i, at, steps) for i, (at, steps) in enumerate(head_streams)),
     ])
@@ -476,7 +476,6 @@
     g = jnp.pad(cotangent, pad)
     full = (images, rows, width)
     thin = (images, rows, local)
-    tall = (images, 2 * rows, width)
     count = lax.axis_size("dp")
     distances = dp_distances(count)
     assert hidden == width and 4 * local == width and 1 << len(distances) == count
@@ -495,39 +494,41 @@
         middle_kernel, 0, "middle", [struct(full, BF16), struct((rows, width), F32)], rows, width,
         [], (part, x, b_proj, ln2_gain, ln2_shift),
     )
-    part, fc, grad_bfc1 = stepped(
+    part, branch, fc, grad_bfc1 = stepped(
         feed_kernel, "feed", images,
         (middle, g, w_fc1, b_fc1, w_fc2),
         [each(full), each(full), fixed((width, hidden)), fixed((hidden,)),
          fixed((hidden, width))],
-        [struct(tall, BF16), struct((width + hidden, width), BF16), struct((1, hidden), F32)],
-        [each(tall), fixed((width + hidden, width)), fixed((1, hidden))],
+        [struct(full, BF16)] * 2
+        + [struct((width + hidden, width), BF16), struct((1, hidden), F32)],
+        [each(full), each(full), fixed((width + hidden, width)), fixed((1, hidden))],
         [pltpu.VMEM((width, hidden), F32), pltpu.VMEM((hidden, width), F32)], 6_000_000_000,
     )
     _, land = streams(width + hidden, count, 4)
-    both, grad_resid, small, fc = exchange(
+    grads_in, grad_resid, small, fc = exchange(
         lambda *refs: turn_kernel(count, *refs), 1, "turn",
-        [struct(tall, BF16), struct((rows, width), F32), struct((8, width), F32),
+        [struct(full, BF16), struct((rows, width), F32), struct((8, width), F32),
          struct(fc.shape, BF16)],
-        2 * rows, width, [pltpu.VMEM((land, width), BF16)],
-        (part, resid, g, b_fc2, ln2_gain, fc),
-    )
-    layer_out = both[:, :length]
+        rows, width, [pltpu.VMEM((land, width), BF16)],
+        (part, resid, g, ln2_gain, fc),
+    )
     _, land = streams(width, count, 2)
-    out, small, fc, heads = exchange(
+    out, small, fc, heads, layer_out = exchange(
         lambda *refs: last_kernel(count, length, *refs), 2, "last",
         [struct(full, BF16), struct((16, width), F32), struct(fc.shape, BF16),
-         struct((width, width), BF16)],
+         struct((width, width), BF16), struct(full, BF16)],
         rows, width,
-        [pltpu.VMEM(full, BF16), pltpu.VMEM((4, local, width), F32),
+        [pltpu.VMEM((2, rows, width), BF16), pltpu.VMEM((rows, width), BF16),
+         pltpu.VMEM((rows, width), BF16), pltpu.VMEM(full, BF16), pltpu.VMEM((4, local, width), F32),
          pltpu.VMEM((2, local), F32), pltpu.VMEM((width, width), BF16),
          pltpu.VMEM((width, width), BF16), pltpu.VMEM((land, width), BF16),
          pltpu.VMEM((3 + len(distances), 16, width), F32),
          pltpu.VMEM((2 + len(distances), 16, width), F32)],
-        (both, mixed, normed, query, keys, values, w_proj, *turned,
-         x, grad_resid, ln1_gain, small, grad_bfc1, fc),
+        (grads_in, mixed, normed, query, keys, values, w_proj, *turned,
+         x, grad_resid, ln1_gain, small, grad_bfc1, fc, branch, resid, b_fc2),
     )
     tokens_grad = out[:, :length]
+    layer_out = layer_out[:, :length]
     heads = heads.astype(F32)
     fc = fc.astype(F32)
     square = lambda i: heads[i * local : (i + 1) * local]

time: 194 us -> 192 us (0.990)
  Pallas kernels: 175 us -> 173 us
where the time goes in v4:
time: 192 us
  Pallas kernels  173 us (90%)
  local copies, waits for them, and re-layouts  17.9 us (9%)
    pallas_call x3, Pallas kernels, exchange(): pl.pallas_call(kernel, out_shape=outs, in_specs=whole(len(args)), out_spe...  152 us
    pallas_call x2, Pallas kernels, stepped(): pl.pallas_call(kernel, grid=(steps,), out_shape=outs, in_specs=arg_specs,...  21.3 us
    unnamed x12, local copies, waits for them, and re-layouts  6.42 us

profile of v4, /device:TPU:0, one launch (start us, length us, event | category | flops | bytes accessed | tf_op | source)
XLA Modules:
  0.0 191.8 jit_solution(15529854040029860062)
XLA Ops:
  0.7 1.4 copy.34
  2.1 0.0 copy-start.2
  2.1 1.1 pad.7.refs_0_.x_ref.refs_10_
  3.2 0.6 copy-done.2
  3.8 0.1 copy.35
  3.9 1.1 pad.8.g_ref.refs_2_
  5.1 9.1 %attention.1 = (bf16[4,208,768]{2,1,0:T(8,128)(2,1)}, bf16[4,208,192]{2,1,0:T(8,128)(2,1)}, bf16[4,208,192]{2,1,0:T(8,128)(2,1)}, bf16[4,208,192]{2,1,0:T(8,128)...) custom-call(bf16[4,208,768]{2,1,0:T(8,128)(2,1)} %pad.7.refs_0_.x_ref.refs_10_, f32[768]{0:T(1024)} %refs_12_.1, ...), custom_call_target="tpu_custom_call" | custom-call | flops 2000000000 | bytes 20000000 | tf_op jit(solution)/shard_map/attention/pallas_call | solution.py:450
  14.1 27.4 %middle.1 = (bf16[4,208,768]{2,1,0:T(8,128)(2,1)}, f32[208,768]{1,0:T(8,128)}) custom-call(bf16[4,208,768]{2,1,0:T(8,128)(2,1)} %get-tuple-element.38.part, bf16[4,208,768]{2,1,0:T(8,128)(2,1)} %pad.7.refs_0_.x_ref.refs_10_, f32[768]{0:T(1024)} %bias.1, f32[768]{0:T(1024)} %refs_3_.3, f32[768]{0:T(1024)} %shift.1), custom_call_target="tpu_custom_call" | custom-call | bytes 50000000 | tf_op jit(solution)/shard_map/middle/pallas_call | solution.py:427
  41.5 12.2 %feed.1 = (bf16[4,208,768]{2,1,0:T(8,128)(2,1)}, bf16[4,208,768]{2,1,0:T(8,128)(2,1)}, bf16[1536,768]{1,0:T(8,128)(2,1)}, f32[1,768]{1,0:T(1,128)}) custom-call(bf16[4,208,768]{2,1,0:T(8,128)(2,1)} %get-tuple-element.39.c_ref, bf16[4,208,768]{2,1,0:T(8,128)(2,1)} %pad.8.g_ref.refs_2_, bf16[768,768]{1,0:T(8,128)(2,1)} %w1.1, f32[768]{0:T(1024)} %b1.1, ...), custom_call_target="tpu_custom_call" | custom-call | flops 6000000000 | bytes 20000000 | tf_op jit(solution)/shard_map/feed/pallas_call | solution.py:450
  53.7 42.8 %turn.1 = (bf16[4,208,768]{2,1,0:T(8,128)(2,1)}, f32[208,768]{1,0:T(8,128)}, f32[8,768]{1,0:T(8,128)}, bf16[1536,768]{1,0:T(8,128)(2,1)}) custom-call(bf16[4,208,768]{2,1,0:T(8,128)(2,1)} %get-tuple-element.40.refs_0_, f32[208,768]{1,0:T(8,128)} %get-tuple-element.41.refs_1_.refs_17_, bf16[4,208,768]{2,1,0:T(8,128)(2,1)} %pad.8.g_ref.refs_2_, f32[768]{0:T(1024)} %refs_3_.3, ...), custom_call_target="tpu_custom_call" | custom-call | bytes 50000000 | tf_op jit(solution)/shard_map/turn/pallas_call | solution.py:427
  96.5 81.5 %last.1 = (bf16[4,208,768]{2,1,0:T(8,128)(2,1)}, f32[16,768]{1,0:T(8,128)}, bf16[1536,768]{1,0:T(8,128)(2,1)}, bf16[768,768]{1,0:T(8,128)(2,1)}, bf16[4,208,768]{2,1,0:T(8,128)(2,1)}) custom-call(bf16[4,208,768]{2,1,0:T(8,128)(2,1)} %get-tuple-element.43.refs_0_, bf16[4,208,192]{2,1,0:T(8,128)(2,1)} %get-tuple-element.44.refs_1_, ...), custom_call_target="tpu_custom_call" | custom-call | bytes 50000000 | tf_op jit(solution)/shard_map/last/pallas_call | solution.py:427
  178.0 1.4 slice.51
  179.4 0.0 copy-start.1
  179.4 1.5 copy.36
  180.9 1.3 fusion.1
  182.3 1.8 slice_reduce_fusion
  184.1 0.0 copy-done.1
  184.1 0.9 slice.71
  184.9 0.2 convert_element_type.9
  185.1 0.0 copy-start.3
  185.1 1.2 slice_bitcast_fusion
  186.3 0.7 copy-done.3
  187.0 0.1 slice.52
  187.1 0.0 copy-start
  187.1 1.5 copy.37
  188.6 0.6 copy-done
  189.2 2.5 %fusion = (f32[768,768]{1,0:T(8,128)}, f32[768,768]{1,0:T(8,128)}) fusion(bf16[1536,768]{1,0:T(8,128)(2,1)S(1)} %copy-done), kind=kLoop, calls=%fused_computation.10 | loop fusion | bytes 9437184 | tf_op jit(solution)/shard_map/slice | solution.py:551
Async XLA Ops:
  2.1 1.7 copy-start.2
  179.4 4.6 %copy-start.1 = (bf16[768,768]{1,0:T(8,128)(2,1)S(1)}, bf16[768,768]{1,0:T(8,128)(2,1)}, u32[]{:S(2)}) copy-start(bf16[768,768]{1,0:T(8,128)(2,1)} %get-tuple-element.57) | copy-start | bytes 3538948
  185.1 1.9 %copy-start.3 = (bf16[4,208,768]{2,1,0:T(8,128)(2,1)S(1)}, bf16[4,208,768]{2,1,0:T(8,128)(2,1)}, u32[]{:S(2)}) copy-start(bf16[4,208,768]{2,1,0:T(8,128)(2,1)} %get-tuple-element.55) | copy-start | bytes 3833860
  187.1 2.1 %copy-start = (bf16[1536,768]{1,0:T(8,128)(2,1)S(1)}, bf16[1536,768]{1,0:T(8,128)(2,1)}, u32[]{:S(2)}) copy-start(bf16[1536,768]{1,0:T(8,128)(2,1)} %get-tuple-element.58) | copy-start | bytes 7077892

commit v5 on v4

--- a/solution.py
+++ b/solution.py
@@ -284,7 +284,7 @@
 
 def streams(rows, count, parts):
     one = dp_distances(count)
-    orders = [one, one[1:] + one[:1]]
+    orders = [one, one[1:2] + one[:1] + one[2:]]
     size = rows // parts
     found, at = [], 0
     for index in range(parts):

time: 192 us -> 189 us (0.984)
  Pallas kernels: 173 us -> 168 us
    pallas_call x3, Pallas kernels: 152 us -> 147 us  [exchange(): pl.pallas_call(kernel, out_shape=outs, in_specs=whole(len(args)), out_spe...]
where the time goes in v5:
time: 189 us; the launch traced here: 187 us
  Pallas kernels  168 us (89%)
  local copies, waits for them, and re-layouts  17.9 us (9%)
    pallas_call x3, Pallas kernels, exchange(): pl.pallas_call(kernel, out_shape=outs, in_specs=whole(len(args)), out_spe...  147 us
    pallas_call x2, Pallas kernels, stepped(): pl.pallas_call(kernel, grid=(steps,), out_shape=outs, in_specs=arg_specs,...  21.3 us
    unnamed x12, local copies, waits for them, and re-layouts  6.42 us

profile of v5, /device:TPU:0, one launch (start us, length us, event | category | flops | bytes accessed | tf_op | source)
XLA Modules:
  0.0 187.2 jit_solution(10705706583721854719)
XLA Ops:
  0.7 1.4 copy.34
  2.1 0.0 copy-start.2
  2.1 1.1 pad.7.refs_0_.x_ref.refs_10_
  3.2 0.6 copy-done.2
  3.8 0.1 copy.35
  3.9 1.1 pad.8.g_ref.refs_2_
  5.1 9.1 %attention.1 = (bf16[4,208,768]{2,1,0:T(8,128)(2,1)}, bf16[4,208,192]{2,1,0:T(8,128)(2,1)}, bf16[4,208,192]{2,1,0:T(8,128)(2,1)}, bf16[4,208,192]{2,1,0:T(8,128)...) custom-call(bf16[4,208,768]{2,1,0:T(8,128)(2,1)} %pad.7.refs_0_.x_ref.refs_10_, f32[768]{0:T(1024)} %refs_12_.1, ...), custom_call_target="tpu_custom_call" | custom-call | flops 2000000000 | bytes 20000000 | tf_op jit(solution)/shard_map/attention/pallas_call | solution.py:450
  14.1 27.4 %middle.1 = (bf16[4,208,768]{2,1,0:T(8,128)(2,1)}, f32[208,768]{1,0:T(8,128)}) custom-call(bf16[4,208,768]{2,1,0:T(8,128)(2,1)} %get-tuple-element.38.part, bf16[4,208,768]{2,1,0:T(8,128)(2,1)} %pad.7.refs_0_.x_ref.refs_10_, f32[768]{0:T(1024)} %bias.1, f32[768]{0:T(1024)} %refs_3_.3, f32[768]{0:T(1024)} %shift.1), custom_call_target="tpu_custom_call" | custom-call | bytes 50000000 | tf_op jit(solution)/shard_map/middle/pallas_call | solution.py:427
  41.5 12.2 %feed.1 = (bf16[4,208,768]{2,1,0:T(8,128)(2,1)}, bf16[4,208,768]{2,1,0:T(8,128)(2,1)}, bf16[1536,768]{1,0:T(8,128)(2,1)}, f32[1,768]{1,0:T(1,128)}) custom-call(bf16[4,208,768]{2,1,0:T(8,128)(2,1)} %get-tuple-element.39.c_ref, bf16[4,208,768]{2,1,0:T(8,128)(2,1)} %pad.8.g_ref.refs_2_, bf16[768,768]{1,0:T(8,128)(2,1)} %w1.1, f32[768]{0:T(1024)} %b1.1, ...), custom_call_target="tpu_custom_call" | custom-call | flops 6000000000 | bytes 20000000 | tf_op jit(solution)/shard_map/feed/pallas_call | solution.py:450
  53.7 41.5 %turn.1 = (bf16[4,208,768]{2,1,0:T(8,128)(2,1)}, f32[208,768]{1,0:T(8,128)}, f32[8,768]{1,0:T(8,128)}, bf16[1536,768]{1,0:T(8,128)(2,1)}) custom-call(bf16[4,208,768]{2,1,0:T(8,128)(2,1)} %get-tuple-element.40.refs_0_, f32[208,768]{1,0:T(8,128)} %get-tuple-element.41.refs_1_.refs_17_, bf16[4,208,768]{2,1,0:T(8,128)(2,1)} %pad.8.g_ref.refs_2_, f32[768]{0:T(1024)} %refs_3_.3, ...), custom_call_target="tpu_custom_call" | custom-call | bytes 50000000 | tf_op jit(solution)/shard_map/turn/pallas_call | solution.py:427
  95.3 78.2 %last.1 = (bf16[4,208,768]{2,1,0:T(8,128)(2,1)}, f32[16,768]{1,0:T(8,128)}, bf16[1536,768]{1,0:T(8,128)(2,1)}, bf16[768,768]{1,0:T(8,128)(2,1)}, bf16[4,208,768]{2,1,0:T(8,128)(2,1)}) custom-call(bf16[4,208,768]{2,1,0:T(8,128)(2,1)} %get-tuple-element.43.refs_0_, bf16[4,208,192]{2,1,0:T(8,128)(2,1)} %get-tuple-element.44.refs_1_, ...), custom_call_target="tpu_custom_call" | custom-call | bytes 50000000 | tf_op jit(solution)/shard_map/last/pallas_call | solution.py:427
  173.5 1.4 slice.51
  174.9 0.0 copy-start.1
  174.9 1.5 copy.36
  176.4 1.3 fusion.1
  177.7 1.8 slice_reduce_fusion
  179.5 0.0 copy-done.1
  179.5 0.9 slice.71
  180.4 0.2 convert_element_type.9
  180.5 0.0 copy-start.3
  180.5 1.2 slice_bitcast_fusion
  181.8 0.7 copy-done.3
  182.5 0.1 slice.52
  182.6 0.0 copy-start
  182.6 1.5 copy.37
  184.1 0.6 copy-done
  184.7 2.5 %fusion = (f32[768,768]{1,0:T(8,128)}, f32[768,768]{1,0:T(8,128)}) fusion(bf16[1536,768]{1,0:T(8,128)(2,1)S(1)} %copy-done), kind=kLoop, calls=%fused_computation.10 | loop fusion | bytes 9437184 | tf_op jit(solution)/shard_map/slice | solution.py:551
Async XLA Ops:
  2.1 1.7 copy-start.2
  174.9 4.6 %copy-start.1 = (bf16[768,768]{1,0:T(8,128)(2,1)S(1)}, bf16[768,768]{1,0:T(8,128)(2,1)}, u32[]{:S(2)}) copy-start(bf16[768,768]{1,0:T(8,128)(2,1)} %get-tuple-element.57) | copy-start | bytes 3538948
  180.5 1.9 %copy-start.3 = (bf16[4,208,768]{2,1,0:T(8,128)(2,1)S(1)}, bf16[4,208,768]{2,1,0:T(8,128)(2,1)}, u32[]{:S(2)}) copy-start(bf16[4,208,768]{2,1,0:T(8,128)(2,1)} %get-tuple-element.55) | copy-start | bytes 3833860
  182.6 2.1 %copy-start = (bf16[1536,768]{1,0:T(8,128)(2,1)S(1)}, bf16[1536,768]{1,0:T(8,128)(2,1)}, u32[]{:S(2)}) copy-start(bf16[1536,768]{1,0:T(8,128)(2,1)} %get-tuple-element.58) | copy-start | bytes 7077892
